TPU v7x, 256 devices: a whole 4x4x8 slice. The times are simulated.
256 devices in a mesh: member: 4 (over z_hi), region: 32 (over z_lo, x, y), fine: 2 (over core).
Axes of the slice: x: 4, y: 4, z: 8 (z_hi: 4, z_lo: 2; z = z_hi * 2 + z_lo), core: 2. Of those that a mesh axis runs over, the one named last changes fastest.
Arguments:
- sample_surface_elevation: float32 [256, 32, 4096], P('member', 'region', 'fine'), may hold values from -6 to 6
- sample_zonal_current: float32 [256, 32, 4096], P('member', 'region', 'fine'), may hold values from -6 to 6
- sample_meridional_current: float32 [256, 32, 4096], P('member', 'region', 'fine'), may hold values from -6 to 6
- zonal_edge_layer_courant: float32 [32, 4096], P('region', 'fine'), may hold values from 0.1 to 0.45
- meridional_edge_layer_courant: float32 [32, 4096], P('region', 'fine'), may hold values from 0.1 to 0.45
- obs_index: int32 [512, 512, 4], P(('member', 'region', 'fine')), may hold values from 0 to 767
- obs_weight: float32 [512, 512, 4], P(('member', 'region', 'fine')), may hold values from 0.1 to 1
- obs_value: float32 [512, 512], P(('member', 'region', 'fine')), may hold values from -12 to 12
- obs_var: float32 [512, 512], P(('member', 'region', 'fine')), may hold values from 0.25 to 4
- obs_count: int32 [512], P(('member', 'region', 'fine')), may hold values from 64 to 512, as said below
- fine_ctrl: float32 [3, 64, 2, 4096], P(None, 'region', 'fine', 'member'), may hold values from -6 to 6
Outputs:
- ana_h: float32 [256, 32, 4096], P('member', 'region', 'fine')
- ana_u: float32 [256, 32, 4096], P('member', 'region', 'fine')
- ana_v: float32 [256, 32, 4096], P('member', 'region', 'fine')
- fine_out: float32 [3, 64, 2, 4096], P(None, 'region', 'fine', 'member')
Inputs may be any that keep to these rules, and one draw needn't show every extreme that they name: `obs_count`: each region's count is 512 // 8 times 1, 2, 4 or 8; some region has 512 and some 512 // 8 in every draw; the live observations of a region are its first count slots.
All inputs are finite; a program needn't handle non-finite values.
Results may differ from a plain program's by a relative error of at most 0.0003.
Values sent between devices are 32-bit elements; how exact they have to be, the bound alone decides.
A program may use at most 64 MiB of HBM per device.

v0:
```python
import functools

import jax
import jax.numpy as jnp
from jax import lax
from jax.experimental import pallas as pl
from jax.experimental.pallas import tpu as pltpu
from jax.sharding import PartitionSpec as P

MESH = pl.DeviceIdType.MESH
STEPS = 4
NEWTON = 8
HIGHEST = lax.Precision.HIGHEST
LANES = 128
MEMS = 64
COLS = 16


def dot(x, y, contract=((1,), (0,))):
    return lax.dot_general(
        x, y, (contract, ((), ())), precision=HIGHEST, preferred_element_type=jnp.float32
    )


def all_sum(x):
    return jnp.sum(jnp.sum(x, axis=1, keepdims=True), axis=0, keepdims=True)


def kernel(
    dims,
    h_ref, u_ref, v_ref, cu_ref, cv_ref, idx_ref, wt_ref, val_ref, var_ref, cnt_ref, fc_ref,
    ah_ref, au_ref, av_ref, fo_ref,
    out_box, in_box, c_out, c_in, to_west, to_east, from_east, from_west,
    state, cour_u, cour_v, stencil, ana, back_out, back_in, inc_out, inc_in,
    out_sem, in_sem, c_out_sem, c_in_sem, halo_sem, back_out_sem, back_in_sem, inc_out_sem,
    inc_in_sem,
):
    n_mem, n_reg = dims
    peers = n_mem * n_reg
    tiles = peers * COLS // LANES
    lane_tiles = n_mem * MEMS // LANES
    members = n_mem * MEMS
    half_rows = n_reg // 2
    cells = half_rows * COLS
    own_tiles = n_reg * COLS // LANES
    a = lax.axis_index("member")
    b = lax.axis_index("region")
    f = lax.axis_index("fine")
    me = a * n_reg + b

    def place(p):
        return (lax.div(p, n_reg), lax.rem(p, n_reg), f)

    ring = f * peers + me
    east = lax.rem(ring + 1, 2 * peers)
    west = lax.rem(ring + 2 * peers - 1, 2 * peers)

    def ring_place(n):
        p = lax.rem(n, peers)
        return (lax.div(p, n_reg), lax.rem(p, n_reg), lax.div(n, peers))

    barrier = pltpu.get_barrier_semaphore()

    def greet(i, carry):
        pl.semaphore_signal(
            barrier, inc=1, device_id=place(lax.rem(me + i, peers)), device_id_type=MESH
        )
        return carry

    lax.fori_loop(1, peers, greet, 0)
    pl.semaphore_signal(barrier, inc=1, device_id=ring_place(east), device_id_type=MESH)
    pl.semaphore_signal(barrier, inc=1, device_id=ring_place(west), device_id_type=MESH)

    lane = lax.broadcasted_iota(jnp.int32, (8, LANES), 1)
    left = lane < MEMS
    wide_lane = lax.broadcasted_iota(jnp.int32, (8, members), 1)
    low = lax.broadcasted_iota(jnp.int32, (8, members), 0) < 4

    def turned(block):
        pair = jnp.concatenate([block, pltpu.roll(block, LANES - 8, axis=1)], axis=0)
        return pair.T

    def pack(j, carry):
        for var, ref in enumerate((h_ref, u_ref, v_ref)):
            t = turned(ref[pl.ds(j, MEMS, stride=tiles), :])
            for k in range(8):
                out_box[j * 8 + k, var] = t[COLS * k : COLS * k + 8]
        return carry

    lax.fori_loop(0, tiles, pack, 0)
    for j in range(own_tiles):
        cu = jnp.broadcast_to(cu_ref[pl.ds(a * own_tiles + j, 1), :], (32, LANES))
        cv = jnp.broadcast_to(cv_ref[pl.ds(a * own_tiles + j, 1), :], (32, LANES))
        t = turned(jnp.concatenate([cu, cv], axis=0))
        for k in range(8):
            c_out[j * 8 + k] = t[COLS * k : COLS * k + 8]

    pl.semaphore_wait(barrier, peers + 1)

    def send_courant(i, carry):
        p = lax.rem(b + i, n_reg)
        pltpu.make_async_remote_copy(
            src_ref=c_out.at[p], dst_ref=c_in.at[b], send_sem=c_out_sem, recv_sem=c_in_sem,
            device_id=(a, p, f), device_id_type=MESH,
        ).start()
        return carry

    def send_state(i, carry):
        p = lax.rem(me + i * 37, peers)
        pltpu.make_async_remote_copy(
            src_ref=out_box.at[p], dst_ref=in_box.at[me], send_sem=out_sem, recv_sem=in_sem,
            device_id=place(p), device_id_type=MESH,
        ).start()
        return carry

    lax.fori_loop(1, n_reg, send_courant, 0)
    lax.fori_loop(1, peers, send_state, 0)
    c_in[b] = c_out[b]
    in_box[me] = out_box[me]

    obs = idx_ref.shape[2]
    for q in range(2):

        def spread_weights(g, carry):
            start = pl.multiple_of(g * 8, 8)
            cell = lax.broadcasted_iota(jnp.int32, (8, obs), 0) + g * 8
            total = jnp.zeros((8, obs), jnp.float32)
            for j in range(4):
                total += jnp.where(idx_ref[q, j : j + 1, :] == cell, wt_ref[q, j : j + 1, :], 0.0)
            stencil[q, pl.ds(start, 8), :] = total
            return carry

        lax.fori_loop(0, 3 * cells // 8, spread_weights, 0)

    def wait_bytes(ref, sem):
        pltpu.make_async_copy(ref, ref, sem).wait()

    wait_bytes(c_in.at[pl.ds(0, n_reg - 1)], c_in_sem)
    wait_bytes(in_box.at[pl.ds(0, peers - 1)], in_sem)

    def assemble(r, carry):
        c = c_in[r]
        for k in range(2):
            cour_u[r, 8 * k : 8 * k + 8] = jnp.broadcast_to(c[:, 64 * k : 64 * k + 1], (8, LANES))
            cour_v[r, 8 * k : 8 * k + 8] = jnp.broadcast_to(
                c[:, 64 * k + 32 : 64 * k + 33], (8, LANES)
            )
        for t in range(lane_tiles):
            at = slice(t * LANES, (t + 1) * LANES)
            for var in range(3):
                x = in_box[2 * t * n_reg + r, var]
                y = in_box[(2 * t + 1) * n_reg + r, var]
                state[var, r, 0:8, at] = jnp.where(left, x, pltpu.roll(y, MEMS, axis=1))
                state[var, r, 8:16, at] = jnp.where(left, pltpu.roll(x, MEMS, axis=1), y)
            c0 = jnp.where(left, cour_u[r, 0:8], cour_v[r, 0:8])
            c1 = jnp.where(left, cour_u[r, 8:16], cour_v[r, 8:16])
            low_t = low[:, at]

            def up(x):
                return pltpu.roll(x, 4, axis=0)

            to_west[r, 0, :, at] = jnp.where(
                low_t, state[0, r, 0:8, at], up(state[1, r, 0:8, at])
            )
            to_west[r, 1, :, at] = jnp.where(low_t, state[2, r, 0:8, at], up(c0))
            to_east[r, 0, :, at] = jnp.where(
                low_t, up(state[1, r, 8:16, at]), state[0, r, 8:16, at]
            )
            to_east[r, 1, :, at] = jnp.where(low_t, up(c1), state[2, r, 8:16, at])
        return carry

    lax.fori_loop(0, n_reg, assemble, 0)
    go_west = pltpu.make_async_remote_copy(
        src_ref=to_west, dst_ref=from_east, send_sem=halo_sem.at[0], recv_sem=halo_sem.at[1],
        device_id=ring_place(west), device_id_type=MESH,
    )
    go_east = pltpu.make_async_remote_copy(
        src_ref=to_east, dst_ref=from_west, send_sem=halo_sem.at[2], recv_sem=halo_sem.at[3],
        device_id=ring_place(east), device_id_type=MESH,
    )
    go_west.start()
    go_east.start()
    go_west.wait_recv()
    go_east.wait_recv()

    def rim(r, carry):
        for t in range(lane_tiles):
            at = slice(t * LANES, (t + 1) * LANES)
            low_t = low[:, at]
            e0, e1 = from_east[r, 0, :, at], from_east[r, 1, :, at]
            w0, w1 = from_west[r, 0, :, at], from_west[r, 1, :, at]
            state[0, r, 16:24, at] = jnp.where(low_t, e0, w0)
            state[1, r, 16:24, at] = pltpu.roll(jnp.where(low_t, w0, e0), 4, axis=0)
            state[2, r, 16:24, at] = jnp.where(low_t, e1, w1)
            if t == 0:
                c = pltpu.roll(jnp.where(low_t, w1, e1), 4, axis=0)
                cour_u[r, 16:24] = jnp.broadcast_to(c[:, 0:1], (8, LANES))
                cour_v[r, 16:24] = jnp.broadcast_to(c[:, 64:65], (8, LANES))
        return carry

    lax.fori_loop(0, n_reg, rim, 0)

    for t in range(lane_tiles):
        at = slice(t * LANES, (t + 1) * LANES)

        def advance(r, carry):
            flux_below, h_below, v_below = carry
            h, u, v = state[0, r, :, at], state[1, r, :, at], state[2, r, :, at]
            flux_u, flux_v = cour_u[r] * u, cour_v[r] * v
            h = h - (flux_u - pltpu.roll(flux_u, 1, axis=0) + flux_v - flux_below)
            state[0, r, :, at] = h
            state[1, r, :, at] = u - (pltpu.roll(h, 23, axis=0) - h)
            state[2, jnp.maximum(r - 1, 0), :, at] = v_below - (h - h_below)
            return flux_v, h, v

        def one_step(s, carry):
            zero = jnp.zeros((24, LANES), jnp.float32)
            _, h, v = lax.fori_loop(0, n_reg, advance, (zero, zero, zero))
            state[2, n_reg - 1, :, at] = v + h
            return carry

        lax.fori_loop(0, STEPS, one_step, 0)

    row_i = lax.broadcasted_iota(jnp.int32, (members, members), 0)
    col_i = lax.broadcasted_iota(jnp.int32, (members, members), 1)
    eye = jnp.where(row_i == col_i, 1.0, 0.0).astype(jnp.float32)
    obs_i = lax.broadcasted_iota(jnp.int32, (1, obs), 1)

    def cells_of(q, var):
        return state[var, q * half_rows : (q + 1) * half_rows, 0:16, :].reshape(cells, members)

    roots, fros, weights, innos = [], [], [], []
    for q in range(2):
        predicted = jnp.zeros((members, obs), jnp.float32)
        for var in range(3):
            predicted += dot(
                cells_of(q, var), stencil[q, var * cells : (var + 1) * cells, :], ((0,), (0,))
            )
        mean_obs = jnp.sum(predicted, axis=0, keepdims=True) / members
        obs_spread = predicted - mean_obs
        active = jnp.where(obs_i < cnt_ref[q], 1.0, 0.0)
        weighted = obs_spread * (active / var_ref[q : q + 1, :])
        scaled = eye + dot(weighted, obs_spread, ((1,), (1,))) / (members - 1)
        fro = jnp.sqrt(all_sum(scaled * scaled))
        iterate = scaled / fro
        factor = 1.5 * eye - 0.5 * iterate
        roots.append((dot(iterate, factor), factor))
        fros.append(fro)
        innos.append(
            jnp.sum(weighted * (val_ref[q : q + 1, :] - mean_obs), axis=1, keepdims=True)
        )

    def sweep(s, carry):
        new = []
        for iterate, root in carry:
            factor = 1.5 * eye - 0.5 * dot(root, iterate)
            new.append((dot(iterate, factor), dot(factor, root)))
        return tuple(new)

    roots = lax.fori_loop(1, NEWTON - 1, sweep, tuple(roots))

    for q in range(2):
        iterate, root = roots[q]
        factor = 1.5 * eye - 0.5 * dot(root, iterate)
        transform = dot(factor, root) / jnp.sqrt(fros[q])
        halfway = jnp.sum(transform * innos[q], axis=0, keepdims=True)
        mean_weights = jnp.sum(transform * halfway, axis=1, keepdims=True) / (members - 1)
        both = jnp.concatenate(
            [transform + mean_weights, jnp.broadcast_to(mean_weights, (members, LANES))], axis=1
        )
        for var in range(3):
            x = cells_of(q, var)
            mean_state = jnp.sum(x, axis=1, keepdims=True) / members
            moved = dot(x - mean_state, both)
            ana[var, :, 0:members] = moved[:, 0:members] + mean_state
            ana[var, :, members:] = moved[:, members:]

        def unload(i, carry):
            lo = pl.multiple_of(i * COLS, 8)
            hi = pl.multiple_of(i * COLS + 8, 8)
            row = q * half_rows + i
            for t in range(lane_tiles):
                at = slice(t * LANES, (t + 1) * LANES)
                for var in range(3):
                    x, y = ana[var, pl.ds(lo, 8), at], ana[var, pl.ds(hi, 8), at]
                    back_out[2 * t * n_reg + row, var] = jnp.where(
                        left, x, pltpu.roll(y, MEMS, axis=1)
                    )
                    back_out[(2 * t + 1) * n_reg + row, var] = jnp.where(
                        left, pltpu.roll(x, MEMS, axis=1), y
                    )
            packed = jnp.zeros((8, LANES), jnp.float32)
            for var in range(3):
                x = ana[var, pl.ds(lo, 8), members:]
                y = ana[var, pl.ds(hi, 8), members:]
                packed = jnp.where(lax.rem(lane, MEMS) // 16 == var, jnp.where(left, x, y), packed)
            inc_out[row] = packed
            return carry

        lax.fori_loop(0, half_rows, unload, 0)

        def send_inc(i, carry):
            p = q * half_rows + lax.rem(b + i, half_rows)

            @pl.when(p != b)
            def _():
                pltpu.make_async_remote_copy(
                    src_ref=inc_out.at[p], dst_ref=inc_in.at[b], send_sem=inc_out_sem,
                    recv_sem=inc_in_sem, device_id=(a, p, f), device_id_type=MESH,
                ).start()

            return carry

        def send_back(i, carry):
            p_mem = lax.rem(a + i, n_mem)
            p_row = q * half_rows + lax.rem(b + lax.div(i, n_mem), half_rows)
            p = p_mem * n_reg + p_row

            @pl.when(p != me)
            def _():
                pltpu.make_async_remote_copy(
                    src_ref=back_out.at[p], dst_ref=back_in.at[me], send_sem=back_out_sem,
                    recv_sem=back_in_sem, device_id=(p_mem, p_row, f), device_id_type=MESH,
                ).start()

            return carry

        lax.fori_loop(0, half_rows, send_inc, 0)
        lax.fori_loop(0, n_mem * half_rows, send_back, 0)

    inc_in[b] = inc_out[b]
    back_in[me] = back_out[me]
    wait_bytes(inc_in.at[pl.ds(0, n_reg - 1)], inc_in_sem)

    def straight(blocks):
        rolled = pltpu.roll(blocks, MEMS, axis=2)
        return jnp.stack([blocks, rolled], axis=1).reshape(LANES, LANES).T

    fine_i = lax.broadcasted_iota(jnp.int32, (LANES, 2 * LANES), 1)
    coarse_i = lax.broadcasted_iota(jnp.int32, (LANES, 2 * LANES), 0)
    widen = jnp.where(lax.div(fine_i, 2) == coarse_i, 1.0, 0.0).astype(jnp.float32)
    for j in range(own_tiles):
        at = slice(2 * j * LANES, 2 * (j + 1) * LANES)
        wide = dot(straight(inc_in[8 * j : 8 * j + 8])[0:64], widen)
        for var in range(3):
            for e in range(2):
                fo_ref[var, e, 0:1, at] = fc_ref[var, e, 0:1, at] + wide[16 * var : 16 * var + 1]

    wait_bytes(back_in.at[pl.ds(0, peers - 1)], back_in_sem)

    def unpack(j, carry):
        for var, ref in enumerate((ah_ref, au_ref, av_ref)):
            start = pl.multiple_of(j * 8, 8)
            blocks = back_in[pl.ds(start, 8), var]
            ref[pl.ds(j, MEMS, stride=tiles), :] = straight(blocks)[0:MEMS]
        return carry

    lax.fori_loop(0, tiles, unpack, 0)

    wait_bytes(c_out.at[pl.ds(0, n_reg - 1)], c_out_sem)
    wait_bytes(out_box.at[pl.ds(0, peers - 1)], out_sem)
    wait_bytes(inc_out.at[pl.ds(0, n_reg - 1)], inc_out_sem)
    wait_bytes(back_out.at[pl.ds(0, peers - 1)], back_out_sem)
    go_west.wait_send()
    go_east.wait_send()


def step(n_mem, n_reg, h, u, v, cu, cv, obs_index, obs_weight, obs_value, obs_var, obs_count, fine):
    peers = n_mem * n_reg
    members = n_mem * MEMS
    tiles = peers * COLS // LANES
    obs = obs_value.shape[1]
    cells = n_reg // 2 * COLS
    f32 = jnp.float32
    flat = (MEMS * tiles, LANES)
    vmem = pl.BlockSpec(memory_space=pltpu.VMEM)
    dma = pltpu.SemaphoreType.DMA
    outs = pl.pallas_call(
        functools.partial(kernel, (n_mem, n_reg)),
        out_shape=[jax.ShapeDtypeStruct(flat, f32)] * 3 + [jax.ShapeDtypeStruct(fine.shape, f32)],
        in_specs=[vmem] * 9 + [pl.BlockSpec(memory_space=pltpu.SMEM), vmem],
        out_specs=[vmem] * 4,
        scratch_shapes=[
            pltpu.VMEM((peers, 3, 8, LANES), f32),
            pltpu.VMEM((peers, 3, 8, LANES), f32),
            pltpu.VMEM((n_reg, 8, LANES), f32),
            pltpu.VMEM((n_reg, 8, LANES), f32),
            pltpu.VMEM((n_reg, 2, 8, members), f32),
            pltpu.VMEM((n_reg, 2, 8, members), f32),
            pltpu.VMEM((n_reg, 2, 8, members), f32),
            pltpu.VMEM((n_reg, 2, 8, members), f32),
            pltpu.VMEM((3, n_reg, 24, members), f32),
            pltpu.VMEM((n_reg, 24, LANES), f32),
            pltpu.VMEM((n_reg, 24, LANES), f32),
            pltpu.VMEM((2, 3 * cells, obs), f32),
            pltpu.VMEM((3, cells, members + LANES), f32),
            pltpu.VMEM((peers, 3, 8, LANES), f32),
            pltpu.VMEM((peers, 3, 8, LANES), f32),
            pltpu.VMEM((n_reg, 8, LANES), f32),
            pltpu.VMEM((n_reg, 8, LANES), f32),
            dma, dma, dma, dma, dma((4,)), dma, dma, dma, dma,
        ],
        compiler_params=pltpu.CompilerParams(
            collective_id=0, has_side_effects=True, vmem_limit_bytes=56 * 1024 * 1024
        ),
    )(
        h.reshape(flat), u.reshape(flat), v.reshape(flat),
        cu.reshape(tiles, LANES), cv.reshape(tiles, LANES),
        obs_index.transpose(0, 2, 1), obs_weight.transpose(0, 2, 1),
        obs_value, obs_var, obs_count, fine,
    )
    return tuple(x.reshape(h.shape) for x in outs[:3]) + (outs[3],)


def solution(mesh):
    fields = P("member", "region", "fine")
    regions = ("member", "region", "fine")
    fine = P(None, "region", "fine", "member")
    return jax.shard_map(
        functools.partial(step, mesh.shape["member"], mesh.shape["region"]),
        mesh=mesh,
        in_specs=(
            fields, fields, fields,
            P("region", "fine"), P("region", "fine"),
            P(regions, None, None), P(regions, None, None),
            P(regions, None), P(regions, None), P(regions),
            fine,
        ),
        out_specs=(fields, fields, fields, fine),
        check_vma=False,
    )
```

profile of v0, /device:TPU:102, one launch (start us, length us, event | category | flops | bytes accessed | tf_op | source)
XLA Modules:
  0.0 144.4 jit_solution(2617502184014564477)
XLA Ops:
  0.6 139.2 %shard_map.138 = (f32[1024,128]{1,0:T(8,128)}, f32[1024,128]{1,0:T(8,128)}, f32[1024,128]{1,0:T(8,128)}, f32[3,2,1,1024]{3,2,1,0:T(1,128)}) custom-call(f32[1024,128]{1,0:T(8,128)} %bitcast.10, f32[1024,128]{1,0:T(8,128)} %bitcast.11, f32[1024,128]{1,0:T(8,128)} %bitcast.12, f32[16,128]{1,0:T(8,128)} %bitcast.18, f32[16,128]{1,0:T(8,128)} %bitcast.19, ...), custom_call_target="tpu_custom_call" | custom-call | tf_op jit(solution)/shard_map/pallas_call | solution.py:378
  139.8 0.0 copy-start.1
  139.8 1.9 %copy.22 = f32[64,1,2048]{2,1,0:T(1,128)} copy(f32[64,1,2048]{2,1,0:T(1,128)} %bitcast.15) | data formatting | bytes 1048576
  141.8 0.0 copy-done.1
  141.8 0.0 copy-start
  141.8 0.8 copy.23
  142.6 0.4 copy-done
  143.0 0.0 copy-start.2
  143.0 0.8 copy.24
  143.8 0.0 copy-done.2
  143.8 0.6 copy.25
Async XLA Ops:
  139.8 1.9 %copy-start.1 = (f32[1024,128]{1,0:T(8,128)S(1)}, f32[1024,128]{1,0:T(8,128)}, u32[]{:S(2)}) copy-start(f32[1024,128]{1,0:T(8,128)} %get-tuple-element.9) | copy-start | bytes 1572868
  141.8 1.2 copy-start
  143.0 0.8 copy-start.2
where the time goes:
time: 147 us; the launch traced here: 144 us
  Pallas kernels  139 us (95%)
  local copies, waits for them, and re-layouts  4.56 us (3%)
    pallas_call x1, Pallas kernels, step(): pl.pallas_call(functools.partial(kernel, (n_mem, n_reg)), out_shape=[jax....  139 us
    unnamed x10, local copies, waits for them, and re-layouts  4.56 us

commit v1 on v0

v1 whole, which is shorter than its diff:
```python
import functools

import jax
import jax.numpy as jnp
from jax import lax
from jax.experimental import pallas as pl
from jax.experimental.pallas import tpu as pltpu
from jax.sharding import PartitionSpec as P

MESH = pl.DeviceIdType.MESH
STEPS = 4
NEWTON = 8
HIGHEST = lax.Precision.HIGHEST
LANES = 128
MEMS = 64
COLS = 16


ROWS_COLS = ((1,), (0,))


def dot(x, y, contract=ROWS_COLS, precision=None):
    return lax.dot_general(
        x, y, (contract, ((), ())), precision=precision, preferred_element_type=jnp.float32
    )


def split(x):
    high = x.astype(jnp.bfloat16)
    return high, (x - high.astype(jnp.float32)).astype(jnp.bfloat16)


def dot3(x, y, contract=ROWS_COLS):
    small = dot(x[0], y[1], contract) + dot(x[1], y[0], contract)
    return dot(x[0], y[0], contract) + small


def all_sum(x):
    return jnp.sum(jnp.sum(x, axis=1, keepdims=True), axis=0, keepdims=True)


def kernel(
    dims,
    h_ref, u_ref, v_ref, cu_ref, cv_ref, idx_ref, wt_ref, val_ref, var_ref, cnt_ref, fc_ref,
    ah_ref, au_ref, av_ref, fo_ref,
    out_box, in_box, c_out, c_in, to_west, to_east, from_east, from_west,
    window, cour_u, cour_v, state, stencil, stencil_hi, stencil_lo, ana,
    back_out, back_in, inc_out, inc_in,
    out_sem, in_sem, c_out_sem, c_in_sem, halo_out_sem, halo_in_sem,
    back_out_sem, back_in_sem, inc_out_sem, inc_in_sem,
):
    n_mem, n_reg = dims
    peers = n_mem * n_reg
    tiles = peers * COLS // LANES
    lane_tiles = n_mem * MEMS // LANES
    members = n_mem * MEMS
    half_rows = n_reg // 2
    cells = half_rows * COLS
    own_tiles = n_reg * COLS // LANES
    phases = [[0], [1, 3], [2]] if n_mem == 4 else [[s] for s in range(n_mem)]
    order = [s for phase in phases for s in phase]
    a = lax.axis_index("member")
    b = lax.axis_index("region")
    f = lax.axis_index("fine")
    me = a * n_reg + b

    def place(p):
        return (lax.div(p, n_reg), lax.rem(p, n_reg), f)

    ring = f * peers + me
    east = lax.rem(ring + 1, 2 * peers)
    west = lax.rem(ring + 2 * peers - 1, 2 * peers)

    def ring_place(n):
        p = lax.rem(n, peers)
        return (lax.div(p, n_reg), lax.rem(p, n_reg), lax.div(n, peers))

    barrier = pltpu.get_barrier_semaphore()

    def greet(i, carry):
        pl.semaphore_signal(
            barrier, inc=1, device_id=place(lax.rem(me + i, peers)), device_id_type=MESH
        )
        return carry

    lax.fori_loop(1, peers, greet, 0)
    pl.semaphore_signal(barrier, inc=1, device_id=ring_place(east), device_id_type=MESH)
    pl.semaphore_signal(barrier, inc=1, device_id=ring_place(west), device_id_type=MESH)

    lane = lax.broadcasted_iota(jnp.int32, (8, LANES), 1)
    left = lane < MEMS
    low = lax.broadcasted_iota(jnp.int32, (8, LANES), 0) < 4
    crossed = (low & ~left) | (~low & left)

    def across(x):
        return pltpu.roll(x, MEMS, axis=1)

    def up(x):
        return pltpu.roll(x, 4, axis=0)

    def turned(block):
        pair = jnp.concatenate([block, pltpu.roll(block, LANES - 8, axis=1)], axis=0)
        return pair.T

    def pack(j, carry):
        for var, ref in enumerate((h_ref, u_ref, v_ref)):
            t = turned(ref[pl.ds(j, MEMS, stride=tiles), :])
            for k in range(8):
                out_box[j * 8 + k, var] = t[COLS * k : COLS * k + 8]
        return carry

    lax.fori_loop(0, tiles, pack, 0)
    for j in range(own_tiles):
        cu = jnp.broadcast_to(cu_ref[pl.ds(a * own_tiles + j, 1), :], (32, LANES))
        cv = jnp.broadcast_to(cv_ref[pl.ds(a * own_tiles + j, 1), :], (32, LANES))
        t = turned(jnp.concatenate([cu, cv], axis=0))
        for k in range(8):
            c_out[j * 8 + k] = t[COLS * k : COLS * k + 8]

    pl.semaphore_wait(barrier, peers + 1)

    def send_courant(i, carry):
        p = lax.rem(b + i, n_reg)
        pltpu.make_async_remote_copy(
            src_ref=c_out.at[p], dst_ref=c_in.at[b], send_sem=c_out_sem, recv_sem=c_in_sem,
            device_id=(a, p, f), device_id_type=MESH,
        ).start()
        return carry

    lax.fori_loop(1, n_reg, send_courant, 0)
    c_in[b] = c_out[b]
    in_box[0, b] = out_box[me]

    for phase in phases:

        def send_state(i, carry):
            p_row = lax.rem(b + i, n_reg)
            for s in phase:
                p_mem = lax.rem(a + s, n_mem)
                slot = (n_mem - s) % n_mem
                pltpu.make_async_remote_copy(
                    src_ref=out_box.at[p_mem * n_reg + p_row], dst_ref=in_box.at[slot, b],
                    send_sem=out_sem, recv_sem=in_sem.at[slot],
                    device_id=(p_mem, p_row, f), device_id_type=MESH,
                ).start()
            return carry

        lax.fori_loop(1 if phase == [0] else 0, n_reg, send_state, 0)

    obs = idx_ref.shape[2]
    for q in range(2):

        def spread_weights(g, carry):
            start = pl.multiple_of(g * 16, 16)
            cell = lax.broadcasted_iota(jnp.int32, (16, obs), 0) + g * 16
            total = jnp.zeros((16, obs), jnp.float32)
            for j in range(4):
                total += jnp.where(idx_ref[q, j : j + 1, :] == cell, wt_ref[q, j : j + 1, :], 0.0)
            high, rest = split(total)
            stencil[q, pl.ds(start, 16), :] = total
            stencil_hi[q, pl.ds(start, 16), :] = high
            stencil_lo[q, pl.ds(start, 16), :] = rest
            return carry

        lax.fori_loop(0, 3 * cells // 16, spread_weights, 0)

    def wait_bytes(ref, sem):
        pltpu.make_async_copy(ref, ref, sem).wait()

    wait_bytes(c_in.at[pl.ds(0, n_reg - 1)], c_in_sem)

    def halo_copies(s):
        there_west = lax.rem(s + a - ring_place(west)[0] + n_mem, n_mem)
        there_east = lax.rem(s + a - ring_place(east)[0] + n_mem, n_mem)
        go_west = pltpu.make_async_remote_copy(
            src_ref=to_west.at[s], dst_ref=from_east.at[there_west],
            send_sem=halo_out_sem.at[0, s], recv_sem=halo_in_sem.at[0, there_west],
            device_id=ring_place(west), device_id_type=MESH,
        )
        go_east = pltpu.make_async_remote_copy(
            src_ref=to_east.at[s], dst_ref=from_west.at[there_east],
            send_sem=halo_out_sem.at[1, s], recv_sem=halo_in_sem.at[1, there_east],
            device_id=ring_place(east), device_id_type=MESH,
        )
        return go_west, go_east

    def send_rim(s):
        wait_bytes(in_box.at[s, pl.ds(0, n_reg - 1 if s == 0 else n_reg)], in_sem.at[s])

        def quarter(r, carry):
            h, u, v = in_box[s, r, 0], in_box[s, r, 1], in_box[s, r, 2]
            c, u = across(c_in[r]), across(u)
            to_west[s, r] = jnp.where(low, jnp.where(left, h, u), up(jnp.where(left, v, c)))
            to_east[s, r] = jnp.where(low, up(jnp.where(left, c, v)), jnp.where(left, u, h))
            return carry

        lax.fori_loop(0, n_reg, quarter, 0, unroll=2)
        for copy in halo_copies(s):
            copy.start()

    def broad(c, at):
        shape = (8, LANES)
        return jnp.where(
            left,
            jnp.broadcast_to(c[:, at : at + 1], shape),
            jnp.broadcast_to(c[:, at + MEMS : at + MEMS + 1], shape),
        )

    def forecast(s):
        wait_bytes(from_east.at[s], halo_in_sem.at[0, s])
        wait_bytes(from_west.at[s], halo_in_sem.at[1, s])

        def rim(r, carry):
            e, w = from_east[s, r], from_west[s, r]
            p, q = jnp.where(low, e, w), up(jnp.where(low, w, e))
            h, u, v = in_box[s, r, 0], in_box[s, r, 1], in_box[s, r, 2]
            window[0, r, 0:8] = h
            window[1, r, 0:8] = u
            window[2, r, 0:8] = v
            window[0, r, 8:16] = across(jnp.where(crossed, h, p))
            window[1, r, 8:16] = jnp.where(crossed, p, across(u))
            window[2, r, 8:16] = across(jnp.where(crossed, v, q))
            if s == 0:
                c = c_in[r]
                cour_u[r, 0:8] = broad(c, 0)
                cour_v[r, 0:8] = broad(c, 32)
                c = jnp.where(crossed, q, across(c))
                cour_u[r, 8:16] = broad(c, 0)
                cour_v[r, 8:16] = broad(c, 32)
            return carry

        lax.fori_loop(0, n_reg, rim, 0, unroll=2)

        def advance(r, carry):
            flux_below, h_below, v_below = carry
            h, u, v = window[0, r], window[1, r], window[2, r]
            flux_u, flux_v = cour_u[r] * u, cour_v[r] * v
            h = h - (flux_u - pltpu.roll(flux_u, 1, axis=0) + flux_v - flux_below)
            window[0, r] = h
            window[1, r] = u - (pltpu.roll(h, 15, axis=0) - h)
            window[2, jnp.maximum(r - 1, 0)] = v_below - (h - h_below)
            return flux_v, h, v

        def one_step(i, carry):
            zero = jnp.zeros((16, LANES), jnp.float32)
            _, h, v = lax.fori_loop(0, n_reg, advance, (zero, zero, zero), unroll=4)
            window[2, n_reg - 1] = v + h
            return carry

        lax.fori_loop(0, STEPS, one_step, 0)
        at = slice(s // 2 * LANES, (s // 2 + 1) * LANES)
        keep = left if s % 2 else ~left

        def place_cells(r, carry):
            for var in range(3):
                x = window[var, r, 0:8]
                y = across(x)
                x, y = (y, x) if s % 2 else (x, y)
                state[var, r, 0:8, at] = jnp.where(keep, state[var, r, 0:8, at], x)
                state[var, r, 8:16, at] = jnp.where(keep, state[var, r, 8:16, at], y)
            return carry

        lax.fori_loop(0, n_reg, place_cells, 0, unroll=2)

    for i, s in enumerate(order):
        send_rim(s)
        if i > 0:
            forecast(order[i - 1])
    forecast(order[-1])

    row_i = lax.broadcasted_iota(jnp.int32, (members, members), 0)
    col_i = lax.broadcasted_iota(jnp.int32, (members, members), 1)
    eye = jnp.where(row_i == col_i, 1.0, 0.0).astype(jnp.float32)
    obs_i = lax.broadcasted_iota(jnp.int32, (1, obs), 1)

    for q in range(2):
        spreads, means = [], []
        obs_spread = jnp.zeros((members, obs), jnp.float32)
        mean_obs = jnp.zeros((1, obs), jnp.float32)
        for var in range(3):
            x = state[var, q * half_rows : (q + 1) * half_rows].reshape(cells, members)
            mean = jnp.sum(x, axis=1, keepdims=True) / members
            spread = split(x - mean)
            block = slice(var * cells, (var + 1) * cells)
            weights = (stencil_hi[q, block, :], stencil_lo[q, block, :])
            obs_spread += dot3(spread, weights, ((0,), (0,)))
            mean_obs += jnp.sum(stencil[q, block, :] * mean, axis=0, keepdims=True)
            spreads.append(spread)
            means.append(mean)
        active = jnp.where(obs_i < cnt_ref[q], 1.0, 0.0)
        weighted = obs_spread * (active / var_ref[q : q + 1, :])
        gram_sum = dot3(split(weighted), split(obs_spread), ((1,), (1,)))
        scaled = eye + gram_sum / (members - 1)
        fro = jnp.sqrt(all_sum(scaled * scaled))
        innovation = jnp.sum(weighted * (val_ref[q : q + 1, :] - mean_obs), axis=1, keepdims=True)
        iterate = scaled / fro
        factor = split(1.5 * eye - 0.5 * iterate)

        def sweep(i, carry):
            iterate, root = carry
            factor = split(1.5 * eye - 0.5 * dot3(root, iterate))
            return split(dot3(iterate, factor)), split(dot3(factor, root))

        iterate, root = lax.fori_loop(
            1, NEWTON - 1, sweep, (split(dot3(split(iterate), factor)), factor)
        )
        factor = split(1.5 * eye - 0.5 * dot3(root, iterate))
        transform = dot3(factor, root) / jnp.sqrt(fro)
        halfway = jnp.sum(transform * innovation, axis=0, keepdims=True)
        mean_weights = jnp.sum(transform * halfway, axis=1, keepdims=True) / (members - 1)
        both = split(jnp.concatenate(
            [transform + mean_weights, jnp.broadcast_to(mean_weights, (members, LANES))], axis=1
        ))
        for var in range(3):
            moved = dot3(spreads[var], both)
            ana[var, :, 0:members] = moved[:, 0:members] + means[var]
            ana[var, :, members:] = moved[:, members:]

        def unload(i, carry):
            lo = pl.multiple_of(i * COLS, 8)
            hi = pl.multiple_of(i * COLS + 8, 8)
            row = q * half_rows + i
            for t in range(lane_tiles):
                at = slice(t * LANES, (t + 1) * LANES)
                for var in range(3):
                    x, y = ana[var, pl.ds(lo, 8), at], ana[var, pl.ds(hi, 8), at]
                    back_out[2 * t, row, var] = jnp.where(left, x, across(y))
                    back_out[2 * t + 1, row, var] = jnp.where(left, across(x), y)
            packed = jnp.zeros((8, LANES), jnp.float32)
            for var in range(3):
                x = ana[var, pl.ds(lo, 8), members:]
                y = ana[var, pl.ds(hi, 8), members:]
                packed = jnp.where(lax.div(lax.rem(lane, MEMS), 16) == var, jnp.where(left, x, y), packed)
            inc_out[row] = packed
            return carry

        lax.fori_loop(0, half_rows, unload, 0, unroll=2)

        def send_inc(i, carry):
            p = q * half_rows + lax.rem(b + i, half_rows)

            @pl.when(p != b)
            def _():
                pltpu.make_async_remote_copy(
                    src_ref=inc_out.at[p], dst_ref=inc_in.at[b], send_sem=inc_out_sem,
                    recv_sem=inc_in_sem, device_id=(a, p, f), device_id_type=MESH,
                ).start()

            return carry

        lax.fori_loop(0, half_rows, send_inc, 0)
        for phase in phases:

            def send_back(i, carry):
                p_row = q * half_rows + lax.rem(b + i, half_rows)
                for s in phase:
                    slot = (n_mem - s) % n_mem
                    copy = pltpu.make_async_remote_copy(
                        src_ref=back_out.at[s, p_row], dst_ref=back_in.at[slot, b],
                        send_sem=back_out_sem, recv_sem=back_in_sem.at[slot],
                        device_id=(lax.rem(a + s, n_mem), p_row, f), device_id_type=MESH,
                    )
                    if s == 0:
                        pl.when(p_row != b)(copy.start)
                    else:
                        copy.start()
                return carry

            lax.fori_loop(0, half_rows, send_back, 0)

    inc_in[b] = inc_out[b]
    back_in[0, b] = back_out[0, b]
    wait_bytes(inc_in.at[pl.ds(0, n_reg - 1)], inc_in_sem)

    def straight(blocks):
        return jnp.stack([blocks, pltpu.roll(blocks, MEMS, axis=2)], axis=1).reshape(LANES, LANES).T

    fine_i = lax.broadcasted_iota(jnp.int32, (LANES, 2 * LANES), 1)
    coarse_i = lax.broadcasted_iota(jnp.int32, (LANES, 2 * LANES), 0)
    widen = jnp.where(lax.div(fine_i, 2) == coarse_i, 1.0, 0.0).astype(jnp.float32)
    for j in range(own_tiles):
        at = slice(2 * j * LANES, 2 * (j + 1) * LANES)
        wide = dot(straight(inc_in[8 * j : 8 * j + 8])[0:64], widen, precision=HIGHEST)
        for var in range(3):
            for e in range(2):
                fo_ref[var, e, 0:1, at] = fc_ref[var, e, 0:1, at] + wide[16 * var : 16 * var + 1]

    for s in order:
        wait_bytes(back_in.at[s, pl.ds(0, n_reg - 1 if s == 0 else n_reg)], back_in_sem.at[s])
        first = lax.rem(a + s, n_mem) * own_tiles

        def unpack(j, carry):
            for var, ref in enumerate((ah_ref, au_ref, av_ref)):
                start = pl.multiple_of(j * 8, 8)
                blocks = back_in[s, pl.ds(start, 8), var]
                ref[pl.ds(first + j, MEMS, stride=tiles), :] = straight(blocks)[0:MEMS]
            return carry

        lax.fori_loop(0, own_tiles, unpack, 0)

    wait_bytes(c_out.at[pl.ds(0, n_reg - 1)], c_out_sem)
    wait_bytes(out_box.at[pl.ds(0, peers - 1)], out_sem)
    wait_bytes(inc_out.at[pl.ds(0, n_reg - 1)], inc_out_sem)
    wait_bytes(out_box.at[pl.ds(0, peers - 1)], back_out_sem)
    for s in order:
        for copy in halo_copies(s):
            copy.wait_send()


def step(n_mem, n_reg, h, u, v, cu, cv, obs_index, obs_weight, obs_value, obs_var, obs_count, fine):
    peers = n_mem * n_reg
    members = n_mem * MEMS
    tiles = peers * COLS // LANES
    obs = obs_value.shape[1]
    cells = n_reg // 2 * COLS
    f32 = jnp.float32
    flat = (MEMS * tiles, LANES)
    vmem = pl.BlockSpec(memory_space=pltpu.VMEM)
    dma = pltpu.SemaphoreType.DMA
    outs = pl.pallas_call(
        functools.partial(kernel, (n_mem, n_reg)),
        out_shape=[jax.ShapeDtypeStruct(flat, f32)] * 3 + [jax.ShapeDtypeStruct(fine.shape, f32)],
        in_specs=[vmem] * 9 + [pl.BlockSpec(memory_space=pltpu.SMEM), vmem],
        out_specs=[vmem] * 4,
        scratch_shapes=[
            pltpu.VMEM((peers, 3, 8, LANES), f32),
            pltpu.VMEM((n_mem, n_reg, 3, 8, LANES), f32),
            pltpu.VMEM((n_reg, 8, LANES), f32),
            pltpu.VMEM((n_reg, 8, LANES), f32),
            pltpu.VMEM((n_mem, n_reg, 8, LANES), f32),
            pltpu.VMEM((n_mem, n_reg, 8, LANES), f32),
            pltpu.VMEM((n_mem, n_reg, 8, LANES), f32),
            pltpu.VMEM((n_mem, n_reg, 8, LANES), f32),
            pltpu.VMEM((3, n_reg, 16, LANES), f32),
            pltpu.VMEM((n_reg, 16, LANES), f32),
            pltpu.VMEM((n_reg, 16, LANES), f32),
            pltpu.VMEM((3, n_reg, 16, members), f32),
            pltpu.VMEM((2, 3 * cells, obs), f32),
            pltpu.VMEM((2, 3 * cells, obs), jnp.bfloat16),
            pltpu.VMEM((2, 3 * cells, obs), jnp.bfloat16),
            pltpu.VMEM((3, cells, members + LANES), f32),
            pltpu.VMEM((n_mem, n_reg, 3, 8, LANES), f32),
            pltpu.VMEM((n_mem, n_reg, 3, 8, LANES), f32),
            pltpu.VMEM((n_reg, 8, LANES), f32),
            pltpu.VMEM((n_reg, 8, LANES), f32),
            dma, dma((n_mem,)), dma, dma, dma((2, n_mem)), dma((2, n_mem)),
            dma, dma((n_mem,)), dma, dma,
        ],
        compiler_params=pltpu.CompilerParams(
            collective_id=0, has_side_effects=True, vmem_limit_bytes=56 * 1024 * 1024
        ),
    )(
        h.reshape(flat), u.reshape(flat), v.reshape(flat),
        cu.reshape(tiles, LANES), cv.reshape(tiles, LANES),
        obs_index.transpose(0, 2, 1), obs_weight.transpose(0, 2, 1),
        obs_value, obs_var, obs_count, fine,
    )
    return tuple(x.reshape(h.shape) for x in outs[:3]) + (outs[3],)


def solution(mesh):
    fields = P("member", "region", "fine")
    regions = ("member", "region", "fine")
    fine = P(None, "region", "fine", "member")
    return jax.shard_map(
        functools.partial(step, mesh.shape["member"], mesh.shape["region"]),
        mesh=mesh,
        in_specs=(
            fields, fields, fields,
            P("region", "fine"), P("region", "fine"),
            P(regions, None, None), P(regions, None, None),
            P(regions, None), P(regions, None), P(regions),
            fine,
        ),
        out_specs=(fields, fields, fields, fine),
        check_vma=False,
    )
```

time: 147 us -> 165 us (1.12); the launches traced: 144 us -> 164 us
  Pallas kernels: 139 us -> 159 us
    pallas_call x1, Pallas kernels: 139 us -> 159 us  [step(): pl.pallas_call(functools.partial(kernel, (n_mem, n_reg)), out_shape=[jax....]
where the time goes in v1:
time: 165 us; the launch traced here: 164 us
  Pallas kernels  159 us (96%)
  local copies, waits for them, and re-layouts  4.56 us (3%)
    pallas_call x1, Pallas kernels, step(): pl.pallas_call(functools.partial(kernel, (n_mem, n_reg)), out_shape=[jax....  159 us
    unnamed x10, local copies, waits for them, and re-layouts  4.56 us

profile of v1, /device:TPU:102, one launch (start us, length us, event | category | flops | bytes accessed | tf_op | source)
XLA Modules:
  0.0 164.3 jit_solution(6292080748854070852)
XLA Ops:
  0.6 159.1 %shard_map.138 = (f32[1024,128]{1,0:T(8,128)}, f32[1024,128]{1,0:T(8,128)}, f32[1024,128]{1,0:T(8,128)}, f32[3,2,1,1024]{3,2,1,0:T(1,128)}) custom-call(f32[1024,128]{1,0:T(8,128)} %bitcast.10, f32[1024,128]{1,0:T(8,128)} %bitcast.11, f32[1024,128]{1,0:T(8,128)} %bitcast.12, f32[16,128]{1,0:T(8,128)} %bitcast.18, f32[16,128]{1,0:T(8,128)} %bitcast.19, ...), custom_call_target="tpu_custom_call" | custom-call | tf_op jit(solution)/shard_map/pallas_call | solution.py:420
  159.7 0.0 copy-start.1
  159.8 1.9 %copy.22 = f32[64,1,2048]{2,1,0:T(1,128)} copy(f32[64,1,2048]{2,1,0:T(1,128)} %bitcast.15) | data formatting | bytes 1048576
  161.7 0.0 copy-done.1
  161.7 0.0 copy-start
  161.7 0.8 copy.23
  162.5 0.4 copy-done
  162.9 0.0 copy-start.2
  162.9 0.8 copy.24
  163.7 0.0 copy-done.2
  163.7 0.6 copy.25
Async XLA Ops:
  159.7 1.9 %copy-start.1 = (f32[1024,128]{1,0:T(8,128)S(1)}, f32[1024,128]{1,0:T(8,128)}, u32[]{:S(2)}) copy-start(f32[1024,128]{1,0:T(8,128)} %get-tuple-element.9) | copy-start | bytes 1572868
  161.7 1.2 copy-start
  162.9 0.8 copy-start.2

commit v2 on v1

--- a/solution.py
+++ b/solution.py
@@ -31,8 +31,10 @@
 
 
 def dot3(x, y, contract=ROWS_COLS):
-    small = dot(x[0], y[1], contract) + dot(x[1], y[0], contract)
-    return dot(x[0], y[0], contract) + small
+    rows = 1 - contract[0][0]
+    size = x[0].shape[rows]
+    both = dot(jnp.concatenate(x, axis=rows), y[0], contract)
+    return both[:size] + (both[size:] + dot(x[0], y[1], contract))
 
 
 def all_sum(x):
@@ -77,13 +79,11 @@
 
     barrier = pltpu.get_barrier_semaphore()
 
-    def greet(i, carry):
+    def greet(i):
         pl.semaphore_signal(
             barrier, inc=1, device_id=place(lax.rem(me + i, peers)), device_id_type=MESH
         )
-        return carry
-
-    lax.fori_loop(1, peers, greet, 0)
+
     pl.semaphore_signal(barrier, inc=1, device_id=ring_place(east), device_id_type=MESH)
     pl.semaphore_signal(barrier, inc=1, device_id=ring_place(west), device_id_type=MESH)
 
@@ -93,23 +93,31 @@
     crossed = (low & ~left) | (~low & left)
 
     def across(x):
-        return pltpu.roll(x, MEMS, axis=1)
+        return pltpu.roll(x, MEMS, axis=x.ndim - 1)
 
     def up(x):
-        return pltpu.roll(x, 4, axis=0)
+        return pltpu.roll(x, 4, axis=x.ndim - 2)
 
     def turned(block):
         pair = jnp.concatenate([block, pltpu.roll(block, LANES - 8, axis=1)], axis=0)
         return pair.T
 
-    def pack(j, carry):
+    def pack_tile(j):
         for var, ref in enumerate((h_ref, u_ref, v_ref)):
             t = turned(ref[pl.ds(j, MEMS, stride=tiles), :])
             for k in range(8):
                 out_box[j * 8 + k, var] = t[COLS * k : COLS * k + 8]
+
+    def pack(j, carry):
+        for k in range(8):
+            greet(j * 8 + k + 1)
+        pack_tile(j)
         return carry
 
-    lax.fori_loop(0, tiles, pack, 0)
+    lax.fori_loop(0, tiles - 1, pack, 0)
+    for k in range(7):
+        greet(peers - 7 + k)
+    pack_tile(tiles - 1)
     for j in range(own_tiles):
         cu = jnp.broadcast_to(cu_ref[pl.ds(a * own_tiles + j, 1), :], (32, LANES))
         cv = jnp.broadcast_to(cv_ref[pl.ds(a * own_tiles + j, 1), :], (32, LANES))
@@ -187,86 +195,100 @@
     def send_rim(s):
         wait_bytes(in_box.at[s, pl.ds(0, n_reg - 1 if s == 0 else n_reg)], in_sem.at[s])
 
-        def quarter(r, carry):
-            h, u, v = in_box[s, r, 0], in_box[s, r, 1], in_box[s, r, 2]
-            c, u = across(c_in[r]), across(u)
-            to_west[s, r] = jnp.where(low, jnp.where(left, h, u), up(jnp.where(left, v, c)))
-            to_east[s, r] = jnp.where(low, up(jnp.where(left, c, v)), jnp.where(left, u, h))
-            return carry
-
-        lax.fori_loop(0, n_reg, quarter, 0, unroll=2)
+        def quarter(i, carry):
+            at = pl.ds(i * 8, 8)
+            h, u, v = in_box[s, at, 0], in_box[s, at, 1], in_box[s, at, 2]
+            c, u = across(c_in[at]), across(u)
+            to_west[s, at] = jnp.where(low, jnp.where(left, h, u), up(jnp.where(left, v, c)))
+            to_east[s, at] = jnp.where(low, up(jnp.where(left, c, v)), jnp.where(left, u, h))
+            return carry
+
+        lax.fori_loop(0, n_reg // 8, quarter, 0)
         for copy in halo_copies(s):
             copy.start()
 
     def broad(c, at):
-        shape = (8, LANES)
         return jnp.where(
             left,
-            jnp.broadcast_to(c[:, at : at + 1], shape),
-            jnp.broadcast_to(c[:, at + MEMS : at + MEMS + 1], shape),
+            jnp.broadcast_to(c[:, :, at : at + 1], c.shape),
+            jnp.broadcast_to(c[:, :, at + MEMS : at + MEMS + 1], c.shape),
         )
 
     def forecast(s):
         wait_bytes(from_east.at[s], halo_in_sem.at[0, s])
         wait_bytes(from_west.at[s], halo_in_sem.at[1, s])
 
-        def rim(r, carry):
-            e, w = from_east[s, r], from_west[s, r]
+        def rim(i, carry):
+            at, to = pl.ds(i * 8, 8), pl.ds(i * 8 + 1, 8)
+            e, w = from_east[s, at], from_west[s, at]
             p, q = jnp.where(low, e, w), up(jnp.where(low, w, e))
-            h, u, v = in_box[s, r, 0], in_box[s, r, 1], in_box[s, r, 2]
-            window[0, r, 0:8] = h
-            window[1, r, 0:8] = u
-            window[2, r, 0:8] = v
-            window[0, r, 8:16] = across(jnp.where(crossed, h, p))
-            window[1, r, 8:16] = jnp.where(crossed, p, across(u))
-            window[2, r, 8:16] = across(jnp.where(crossed, v, q))
+            h, u, v = in_box[s, at, 0], in_box[s, at, 1], in_box[s, at, 2]
+            window[0, to, 0:8] = h
+            window[1, to, 0:8] = u
+            window[2, to, 0:8] = v
+            window[0, to, 8:16] = across(jnp.where(crossed, h, p))
+            window[1, to, 8:16] = jnp.where(crossed, p, across(u))
+            window[2, to, 8:16] = across(jnp.where(crossed, v, q))
             if s == 0:
-                c = c_in[r]
-                cour_u[r, 0:8] = broad(c, 0)
-                cour_v[r, 0:8] = broad(c, 32)
+                c = c_in[at]
+                cour_u[to, 0:8] = broad(c, 0)
+                cour_v[to, 0:8] = broad(c, 32)
                 c = jnp.where(crossed, q, across(c))
-                cour_u[r, 8:16] = broad(c, 0)
-                cour_v[r, 8:16] = broad(c, 32)
-            return carry
-
-        lax.fori_loop(0, n_reg, rim, 0, unroll=2)
-
-        def advance(r, carry):
-            flux_below, h_below, v_below = carry
-            h, u, v = window[0, r], window[1, r], window[2, r]
-            flux_u, flux_v = cour_u[r] * u, cour_v[r] * v
-            h = h - (flux_u - pltpu.roll(flux_u, 1, axis=0) + flux_v - flux_below)
-            window[0, r] = h
-            window[1, r] = u - (pltpu.roll(h, 15, axis=0) - h)
-            window[2, jnp.maximum(r - 1, 0)] = v_below - (h - h_below)
-            return flux_v, h, v
+                cour_u[to, 8:16] = broad(c, 0)
+                cour_v[to, 8:16] = broad(c, 32)
+            return carry
+
+        lax.fori_loop(0, n_reg // 8, rim, 0)
+
+        def heights(i, carry):
+            at = pl.ds(i * 8 + 1, 8)
+            flux_u = cour_u[at] * window[1, at]
+            flux_v = cour_v[pl.ds(i * 8, 9)] * window[2, pl.ds(i * 8, 9)]
+            gain = flux_u - pltpu.roll(flux_u, 1, axis=1) + flux_v[1:] - flux_v[:-1]
+            window[0, at] = window[0, at] - gain
+            return carry
+
+        def currents(i, carry):
+            at = pl.ds(i * 8 + 1, 8)
+            h = window[0, pl.ds(i * 8 + 1, 9)]
+            window[1, at] = window[1, at] - (pltpu.roll(h[:-1], 15, axis=1) - h[:-1])
+            window[2, at] = window[2, at] - (h[1:] - h[:-1])
+            return carry
 
         def one_step(i, carry):
-            zero = jnp.zeros((16, LANES), jnp.float32)
-            _, h, v = lax.fori_loop(0, n_reg, advance, (zero, zero, zero), unroll=4)
-            window[2, n_reg - 1] = v + h
+            lax.fori_loop(0, n_reg // 8, heights, 0, unroll=True)
+            lax.fori_loop(0, n_reg // 8, currents, 0, unroll=True)
             return carry
 
         lax.fori_loop(0, STEPS, one_step, 0)
-        at = slice(s // 2 * LANES, (s // 2 + 1) * LANES)
+        tile = slice(s // 2 * LANES, (s // 2 + 1) * LANES)
         keep = left if s % 2 else ~left
 
-        def place_cells(r, carry):
+        def place_cells(i, carry):
+            at = pl.ds(i * 8, 8)
             for var in range(3):
-                x = window[var, r, 0:8]
+                x = window[var, pl.ds(i * 8 + 1, 8), 0:8]
                 y = across(x)
                 x, y = (y, x) if s % 2 else (x, y)
-                state[var, r, 0:8, at] = jnp.where(keep, state[var, r, 0:8, at], x)
-                state[var, r, 8:16, at] = jnp.where(keep, state[var, r, 8:16, at], y)
-            return carry
-
-        lax.fori_loop(0, n_reg, place_cells, 0, unroll=2)
-
-    for i, s in enumerate(order):
+                state[var, at, 0:8, tile] = jnp.where(keep, state[var, at, 0:8, tile], x)
+                state[var, at, 8:16, tile] = jnp.where(keep, state[var, at, 8:16, tile], y)
+            return carry
+
+        lax.fori_loop(0, n_reg // 8, place_cells, 0)
+
+    blank = jnp.zeros((16, LANES), jnp.float32)
+    window[0, n_reg + 1] = blank
+    window[2, 0] = blank
+    cour_v[0] = blank
+
+    early = order[:-1] if n_mem > 2 else order
+    for s in early:
         send_rim(s)
-        if i > 0:
-            forecast(order[i - 1])
-    forecast(order[-1])
+    forecast(order[0])
+    for s in order[len(early) :]:
+        send_rim(s)
+    for s in order[1:]:
+        forecast(s)
 
     row_i = lax.broadcasted_iota(jnp.int32, (members, members), 0)
     col_i = lax.broadcasted_iota(jnp.int32, (members, members), 1)
@@ -431,9 +453,9 @@
             pltpu.VMEM((n_mem, n_reg, 8, LANES), f32),
             pltpu.VMEM((n_mem, n_reg, 8, LANES), f32),
             pltpu.VMEM((n_mem, n_reg, 8, LANES), f32),
-            pltpu.VMEM((3, n_reg, 16, LANES), f32),
-            pltpu.VMEM((n_reg, 16, LANES), f32),
-            pltpu.VMEM((n_reg, 16, LANES), f32),
+            pltpu.VMEM((3, n_reg + 2, 16, LANES), f32),
+            pltpu.VMEM((n_reg + 2, 16, LANES), f32),
+            pltpu.VMEM((n_reg + 2, 16, LANES), f32),
             pltpu.VMEM((3, n_reg, 16, members), f32),
             pltpu.VMEM((2, 3 * cells, obs), f32),
             pltpu.VMEM((2, 3 * cells, obs), jnp.bfloat16),

time: 165 us -> 126 us (0.76)
  Pallas kernels: 159 us -> 121 us
    pallas_call x1, Pallas kernels: 159 us -> 121 us  [step(): pl.pallas_call(functools.partial(kernel, (n_mem, n_reg)), out_shape=[jax....]
where the time goes in v2:
time: 126 us
  Pallas kernels  121 us (96%)
  local copies, waits for them, and re-layouts  4.56 us (4%)
    pallas_call x1, Pallas kernels, step(): pl.pallas_call(functools.partial(kernel, (n_mem, n_reg)), out_shape=[jax....  121 us
    unnamed x10, local copies, waits for them, and re-layouts  4.56 us

profile of v2, /device:TPU:102, one launch (start us, length us, event | category | flops | bytes accessed | tf_op | source)
XLA Modules:
  0.0 126.1 jit_solution(10421059576099808583)
XLA Ops:
  0.6 120.8 %shard_map.138 = (f32[1024,128]{1,0:T(8,128)}, f32[1024,128]{1,0:T(8,128)}, f32[1024,128]{1,0:T(8,128)}, f32[3,2,1,1024]{3,2,1,0:T(1,128)}) custom-call(f32[1024,128]{1,0:T(8,128)} %bitcast.10, f32[1024,128]{1,0:T(8,128)} %bitcast.11, f32[1024,128]{1,0:T(8,128)} %bitcast.12, f32[16,128]{1,0:T(8,128)} %bitcast.18, f32[16,128]{1,0:T(8,128)} %bitcast.19, ...), custom_call_target="tpu_custom_call" | custom-call | tf_op jit(solution)/shard_map/pallas_call | solution.py:442
  121.5 0.0 copy-start.1
  121.5 1.9 %copy.22 = f32[64,1,2048]{2,1,0:T(1,128)} copy(f32[64,1,2048]{2,1,0:T(1,128)} %bitcast.15) | data formatting | bytes 1048576
  123.4 0.0 copy-done.1
  123.4 0.0 copy-start
  123.4 0.8 copy.23
  124.2 0.4 copy-done
  124.7 0.0 copy-start.2
  124.7 0.8 copy.24
  125.5 0.0 copy-done.2
  125.5 0.6 copy.25
Async XLA Ops:
  121.5 1.9 %copy-start.1 = (f32[1024,128]{1,0:T(8,128)S(1)}, f32[1024,128]{1,0:T(8,128)}, u32[]{:S(2)}) copy-start(f32[1024,128]{1,0:T(8,128)} %get-tuple-element.9) | copy-start | bytes 1572868
  123.4 1.2 copy-start
  124.7 0.8 copy-start.2

commit v3 on v2

--- a/solution.py
+++ b/solution.py
@@ -47,9 +47,9 @@
     ah_ref, au_ref, av_ref, fo_ref,
     out_box, in_box, c_out, c_in, to_west, to_east, from_east, from_west,
     window, cour_u, cour_v, state, stencil, stencil_hi, stencil_lo, ana,
-    back_out, back_in, inc_out, inc_in,
+    back_out, back_in, inc_out, inc_in, h_in, u_in, v_in, c_edge, edges,
     out_sem, in_sem, c_out_sem, c_in_sem, halo_out_sem, halo_in_sem,
-    back_out_sem, back_in_sem, inc_out_sem, inc_in_sem,
+    back_out_sem, back_in_sem, inc_out_sem, inc_in_sem, load_sem, edge_sem,
 ):
     n_mem, n_reg = dims
     peers = n_mem * n_reg
@@ -59,6 +59,7 @@
     half_rows = n_reg // 2
     cells = half_rows * COLS
     own_tiles = n_reg * COLS // LANES
+    plane = n_reg // 2
     phases = [[0], [1, 3], [2]] if n_mem == 4 else [[s] for s in range(n_mem)]
     order = [s for phase in phases for s in phase]
     a = lax.axis_index("member")
@@ -69,23 +70,33 @@
     def place(p):
         return (lax.div(p, n_reg), lax.rem(p, n_reg), f)
 
-    ring = f * peers + me
-    east = lax.rem(ring + 1, 2 * peers)
-    west = lax.rem(ring + 2 * peers - 1, 2 * peers)
-
-    def ring_place(n):
-        p = lax.rem(n, peers)
-        return (lax.div(p, n_reg), lax.rem(p, n_reg), lax.div(n, peers))
+    loads = [
+        pltpu.make_async_copy(ref, box, load_sem.at[i])
+        for i, (ref, box) in enumerate(((h_ref, h_in), (u_ref, u_in), (v_ref, v_in)))
+    ]
+    for load in loads:
+        load.start()
 
     barrier = pltpu.get_barrier_semaphore()
 
-    def greet(i):
+    def greet(i, carry):
         pl.semaphore_signal(
             barrier, inc=1, device_id=place(lax.rem(me + i, peers)), device_id_type=MESH
         )
-
-    pl.semaphore_signal(barrier, inc=1, device_id=ring_place(east), device_id_type=MESH)
-    pl.semaphore_signal(barrier, inc=1, device_id=ring_place(west), device_id_type=MESH)
+        return carry
+
+    def greet_other_half(i, carry):
+        p_mem, p_row, _ = place(i)
+        pl.semaphore_signal(barrier, inc=1, device_id=(p_mem, p_row, 1 - f), device_id_type=MESH)
+        return carry
+
+    @pl.when((me == 0) | (me == peers - 1))
+    def _():
+        lax.fori_loop(0, peers, greet_other_half, 0)
+
+    lax.fori_loop(1, peers, greet, 0)
+    for load in loads:
+        load.wait()
 
     lane = lax.broadcasted_iota(jnp.int32, (8, LANES), 1)
     left = lane < MEMS
@@ -102,28 +113,43 @@
         pair = jnp.concatenate([block, pltpu.roll(block, LANES - 8, axis=1)], axis=0)
         return pair.T
 
-    def pack_tile(j):
-        for var, ref in enumerate((h_ref, u_ref, v_ref)):
+    def pack(j, carry):
+        for var, ref in enumerate((h_in, u_in, v_in)):
             t = turned(ref[pl.ds(j, MEMS, stride=tiles), :])
             for k in range(8):
                 out_box[j * 8 + k, var] = t[COLS * k : COLS * k + 8]
-
-    def pack(j, carry):
-        for k in range(8):
-            greet(j * 8 + k + 1)
-        pack_tile(j)
         return carry
 
-    lax.fori_loop(0, tiles - 1, pack, 0)
-    for k in range(7):
-        greet(peers - 7 + k)
-    pack_tile(tiles - 1)
+    lax.fori_loop(0, tiles, pack, 0)
+
+    def courant(j):
+        cu = jnp.broadcast_to(cu_ref[pl.ds(j, 1), :], (32, LANES))
+        cv = jnp.broadcast_to(cv_ref[pl.ds(j, 1), :], (32, LANES))
+        return turned(jnp.concatenate([cu, cv], axis=0))
+
+    def west_going(h, u, v, c):
+        c, u = across(c), across(u)
+        return jnp.where(low, jnp.where(left, h, u), up(jnp.where(left, v, c)))
+
+    def east_going(h, u, v, c):
+        c, u = across(c), across(u)
+        return jnp.where(low, up(jnp.where(left, c, v)), jnp.where(left, u, h))
+
     for j in range(own_tiles):
-        cu = jnp.broadcast_to(cu_ref[pl.ds(a * own_tiles + j, 1), :], (32, LANES))
-        cv = jnp.broadcast_to(cv_ref[pl.ds(a * own_tiles + j, 1), :], (32, LANES))
-        t = turned(jnp.concatenate([cu, cv], axis=0))
+        t = courant(a * own_tiles + j)
         for k in range(8):
             c_out[j * 8 + k] = t[COLS * k : COLS * k + 8]
+
+    c_edge[0] = courant(lax.rem(a + 1, n_mem) * own_tiles)[0:8]
+    c_edge[1] = courant(lax.rem(a * own_tiles + tiles - 1, tiles))[7 * COLS : 7 * COLS + 8]
+    for k in range(n_mem):
+        for kind, (m, c, going) in enumerate((
+            (k * n_reg + plane, c_out[plane], west_going),
+            ((k + 1) % n_mem * n_reg, c_edge[0], west_going),
+            (k * n_reg + plane - 1, c_out[plane - 1], east_going),
+            ((k * n_reg + peers - 1) % peers, c_edge[1], east_going),
+        )):
+            edges[k, kind] = going(out_box[m, 0], out_box[m, 1], out_box[m, 2], c)
 
     pl.semaphore_wait(barrier, peers + 1)
 
@@ -154,6 +180,29 @@
             return carry
 
         lax.fori_loop(1 if phase == [0] else 0, n_reg, send_state, 0)
+        for s in phase:
+            p_mem = lax.rem(a + s, n_mem)
+            slot = (n_mem - s) % n_mem
+            for kind, (p_row, box, other) in enumerate((
+                (plane - 1, from_east, None),
+                (n_reg - 1, from_east, n_mem - 1),
+                (plane, from_west, None),
+                (0, from_west, 0),
+            )):
+                here = f if other is None else jnp.where(p_mem == other, 1 - f, f)
+                sem = halo_in_sem.at[kind // 2, slot]
+                go = pltpu.make_async_remote_copy(
+                    src_ref=edges.at[p_mem, kind], dst_ref=box.at[slot, b],
+                    send_sem=edge_sem, recv_sem=sem,
+                    device_id=(p_mem, p_row, here), device_id_type=MESH,
+                )
+                if s:
+                    go.start()
+                else:
+                    own = (b == p_row) if other is None else (b == p_row) & (a != other)
+                    stay = pltpu.make_async_copy(edges.at[p_mem, kind], box.at[slot, b], sem)
+                    pl.when(own)(stay.start)
+                    pl.when(jnp.logical_not(own))(go.start)
 
     obs = idx_ref.shape[2]
     for q in range(2):
@@ -177,20 +226,21 @@
 
     wait_bytes(c_in.at[pl.ds(0, n_reg - 1)], c_in_sem)
 
+    inside_west = lax.rem(b, plane) != 0
+    inside_east = lax.rem(b, plane) != plane - 1
+
     def halo_copies(s):
-        there_west = lax.rem(s + a - ring_place(west)[0] + n_mem, n_mem)
-        there_east = lax.rem(s + a - ring_place(east)[0] + n_mem, n_mem)
         go_west = pltpu.make_async_remote_copy(
-            src_ref=to_west.at[s], dst_ref=from_east.at[there_west],
-            send_sem=halo_out_sem.at[0, s], recv_sem=halo_in_sem.at[0, there_west],
-            device_id=ring_place(west), device_id_type=MESH,
+            src_ref=to_west.at[s], dst_ref=from_east.at[s],
+            send_sem=halo_out_sem.at[0, s], recv_sem=halo_in_sem.at[0, s],
+            device_id=(a, lax.rem(b + n_reg - 1, n_reg), f), device_id_type=MESH,
         )
         go_east = pltpu.make_async_remote_copy(
-            src_ref=to_east.at[s], dst_ref=from_west.at[there_east],
-            send_sem=halo_out_sem.at[1, s], recv_sem=halo_in_sem.at[1, there_east],
-            device_id=ring_place(east), device_id_type=MESH,
+            src_ref=to_east.at[s], dst_ref=from_west.at[s],
+            send_sem=halo_out_sem.at[1, s], recv_sem=halo_in_sem.at[1, s],
+            device_id=(a, lax.rem(b + 1, n_reg), f), device_id_type=MESH,
         )
-        return go_west, go_east
+        return (inside_west, go_west), (inside_east, go_east)
 
     def send_rim(s):
         wait_bytes(in_box.at[s, pl.ds(0, n_reg - 1 if s == 0 else n_reg)], in_sem.at[s])
@@ -198,14 +248,14 @@
         def quarter(i, carry):
             at = pl.ds(i * 8, 8)
             h, u, v = in_box[s, at, 0], in_box[s, at, 1], in_box[s, at, 2]
-            c, u = across(c_in[at]), across(u)
-            to_west[s, at] = jnp.where(low, jnp.where(left, h, u), up(jnp.where(left, v, c)))
-            to_east[s, at] = jnp.where(low, up(jnp.where(left, c, v)), jnp.where(left, u, h))
+            c = c_in[at]
+            to_west[s, at] = west_going(h, u, v, c)
+            to_east[s, at] = east_going(h, u, v, c)
             return carry
 
         lax.fori_loop(0, n_reg // 8, quarter, 0)
-        for copy in halo_copies(s):
-            copy.start()
+        for inside, copy in halo_copies(s):
+            pl.when(inside)(copy.start)
 
     def broad(c, at):
         return jnp.where(
@@ -281,12 +331,10 @@
     window[2, 0] = blank
     cour_v[0] = blank
 
-    early = order[:-1] if n_mem > 2 else order
-    for s in early:
+    for s in order[:-1]:
         send_rim(s)
     forecast(order[0])
-    for s in order[len(early) :]:
-        send_rim(s)
+    send_rim(order[-1])
     for s in order[1:]:
         forecast(s)
 
@@ -324,7 +372,7 @@
             return split(dot3(iterate, factor)), split(dot3(factor, root))
 
         iterate, root = lax.fori_loop(
-            1, NEWTON - 1, sweep, (split(dot3(split(iterate), factor)), factor)
+            1, NEWTON - 1, sweep, (split(dot3(split(iterate), factor)), factor), unroll=2
         )
         factor = split(1.5 * eye - 0.5 * dot3(root, iterate))
         transform = dot3(factor, root) / jnp.sqrt(fro)
@@ -339,6 +387,7 @@
             ana[var, :, members:] = moved[:, members:]
 
         def unload(i, carry):
+            i = lax.rem(b + i, half_rows)
             lo = pl.multiple_of(i * COLS, 8)
             hi = pl.multiple_of(i * COLS + 8, 8)
             row = q * half_rows + i
@@ -354,41 +403,44 @@
                 y = ana[var, pl.ds(hi, 8), members:]
                 packed = jnp.where(lax.div(lax.rem(lane, MEMS), 16) == var, jnp.where(left, x, y), packed)
             inc_out[row] = packed
-            return carry
-
-        lax.fori_loop(0, half_rows, unload, 0, unroll=2)
-
-        def send_inc(i, carry):
-            p = q * half_rows + lax.rem(b + i, half_rows)
-
-            @pl.when(p != b)
-            def _():
-                pltpu.make_async_remote_copy(
-                    src_ref=inc_out.at[p], dst_ref=inc_in.at[b], send_sem=inc_out_sem,
-                    recv_sem=inc_in_sem, device_id=(a, p, f), device_id_type=MESH,
-                ).start()
-
-            return carry
-
-        lax.fori_loop(0, half_rows, send_inc, 0)
-        for phase in phases:
-
-            def send_back(i, carry):
-                p_row = q * half_rows + lax.rem(b + i, half_rows)
-                for s in phase:
-                    slot = (n_mem - s) % n_mem
-                    copy = pltpu.make_async_remote_copy(
-                        src_ref=back_out.at[s, p_row], dst_ref=back_in.at[slot, b],
-                        send_sem=back_out_sem, recv_sem=back_in_sem.at[slot],
-                        device_id=(lax.rem(a + s, n_mem), p_row, f), device_id_type=MESH,
-                    )
-                    if s == 0:
-                        pl.when(p_row != b)(copy.start)
-                    else:
-                        copy.start()
-                return carry
-
-            lax.fori_loop(0, half_rows, send_back, 0)
+            if q == 0:
+                send_inc(row)
+                for s in order:
+                    send_back(s, row)
+            return carry
+
+        def send_inc(row):
+            go = pltpu.make_async_remote_copy(
+                src_ref=inc_out.at[row], dst_ref=inc_in.at[b], send_sem=inc_out_sem,
+                recv_sem=inc_in_sem, device_id=(a, row, f), device_id_type=MESH,
+            )
+            pl.when(row != b)(go.start)
+
+        def send_back(s, row):
+            slot = (n_mem - s) % n_mem
+            go = pltpu.make_async_remote_copy(
+                src_ref=back_out.at[s, row], dst_ref=back_in.at[slot, b],
+                send_sem=back_out_sem, recv_sem=back_in_sem.at[slot],
+                device_id=(lax.rem(a + s, n_mem), row, f), device_id_type=MESH,
+            )
+            if s:
+                go.start()
+            else:
+                pl.when(row != b)(go.start)
+
+        lax.fori_loop(0, half_rows, unload, 0)
+        if q:
+            for phase in phases:
+
+                def send_phase(i, carry):
+                    row = q * half_rows + lax.rem(b + i, half_rows)
+                    if phase == phases[0]:
+                        send_inc(row)
+                    for s in phase:
+                        send_back(s, row)
+                    return carry
+
+                lax.fori_loop(0, half_rows, send_phase, 0)
 
     inc_in[b] = inc_out[b]
     back_in[0, b] = back_out[0, b]
@@ -425,8 +477,19 @@
     wait_bytes(inc_out.at[pl.ds(0, n_reg - 1)], inc_out_sem)
     wait_bytes(out_box.at[pl.ds(0, peers - 1)], back_out_sem)
     for s in order:
-        for copy in halo_copies(s):
-            copy.wait_send()
+        for inside, copy in halo_copies(s):
+            pl.when(inside)(copy.wait_send)
+
+    own_edge = (b == plane - 1) | (b == plane)
+    own_edge |= ((b == n_reg - 1) & (a != n_mem - 1)) | ((b == 0) & (a != 0))
+
+    @pl.when(own_edge)
+    def _():
+        wait_bytes(c_out.at[pl.ds(0, 4 * n_mem - 1)], edge_sem)
+
+    @pl.when(jnp.logical_not(own_edge))
+    def _():
+        wait_bytes(c_out.at[pl.ds(0, 4 * n_mem)], edge_sem)
 
 
 def step(n_mem, n_reg, h, u, v, cu, cv, obs_index, obs_weight, obs_value, obs_var, obs_count, fine):
@@ -442,7 +505,7 @@
     outs = pl.pallas_call(
         functools.partial(kernel, (n_mem, n_reg)),
         out_shape=[jax.ShapeDtypeStruct(flat, f32)] * 3 + [jax.ShapeDtypeStruct(fine.shape, f32)],
-        in_specs=[vmem] * 9 + [pl.BlockSpec(memory_space=pltpu.SMEM), vmem],
+        in_specs=[pl.BlockSpec(memory_space=pl.ANY)] * 3 + [vmem] * 6 + [pl.BlockSpec(memory_space=pltpu.SMEM), vmem],
         out_specs=[vmem] * 4,
         scratch_shapes=[
             pltpu.VMEM((peers, 3, 8, LANES), f32),
@@ -465,8 +528,11 @@
             pltpu.VMEM((n_mem, n_reg, 3, 8, LANES), f32),
             pltpu.VMEM((n_reg, 8, LANES), f32),
             pltpu.VMEM((n_reg, 8, LANES), f32),
+            pltpu.VMEM(flat, f32), pltpu.VMEM(flat, f32), pltpu.VMEM(flat, f32),
+            pltpu.VMEM((2, 8, LANES), f32),
+            pltpu.VMEM((n_mem, 4, 8, LANES), f32),
             dma, dma((n_mem,)), dma, dma, dma((2, n_mem)), dma((2, n_mem)),
-            dma, dma((n_mem,)), dma, dma,
+            dma, dma((n_mem,)), dma, dma, dma((3,)), dma,
         ],
         compiler_params=pltpu.CompilerParams(
             collective_id=0, has_side_effects=True, vmem_limit_bytes=56 * 1024 * 1024

time: 126 us -> 116 us (0.921)
  Pallas kernels: 121 us -> 110 us
    pallas_call x1, Pallas kernels: 121 us -> 110 us  [step(): pl.pallas_call(functools.partial(kernel, (n_mem, n_reg)), out_shape=[jax....]
where the time goes in v3:
time: 116 us; the launch traced here: 115 us
  Pallas kernels  110 us (95%)
  local copies, waits for them, and re-layouts  4.56 us (4%)
    pallas_call x1, Pallas kernels, step(): pl.pallas_call(functools.partial(kernel, (n_mem, n_reg)), out_shape=[jax....  110 us
    unnamed x10, local copies, waits for them, and re-layouts  4.56 us

profile of v3, /device:TPU:102, one launch (start us, length us, event | category | flops | bytes accessed | tf_op | source)
XLA Modules:
  0.0 115.4 jit_solution(13051466635141980353)
XLA Ops:
  0.6 110.2 %shard_map.138 = (f32[1024,128]{1,0:T(8,128)}, f32[1024,128]{1,0:T(8,128)}, f32[1024,128]{1,0:T(8,128)}, f32[3,2,1,1024]{3,2,1,0:T(1,128)}) custom-call(f32[1024,128]{1,0:T(8,128)} %bitcast.10, f32[1024,128]{1,0:T(8,128)} %bitcast.11, f32[1024,128]{1,0:T(8,128)} %bitcast.12, f32[16,128]{1,0:T(8,128)} %bitcast.18, f32[16,128]{1,0:T(8,128)} %bitcast.19, ...), custom_call_target="tpu_custom_call" | custom-call | tf_op jit(solution)/shard_map/pallas_call | solution.py:505
  110.8 0.0 copy-start.1
  110.8 1.9 %copy.22 = f32[64,1,2048]{2,1,0:T(1,128)} copy(f32[64,1,2048]{2,1,0:T(1,128)} %bitcast.15) | data formatting | bytes 1048576
  112.8 0.0 copy-done.1
  112.8 0.0 copy-start
  112.8 0.8 copy.23
  113.6 0.4 copy-done
  114.0 0.0 copy-start.2
  114.0 0.8 copy.24
  114.8 0.0 copy-done.2
  114.8 0.6 copy.25
Async XLA Ops:
  110.8 1.9 %copy-start.1 = (f32[1024,128]{1,0:T(8,128)S(1)}, f32[1024,128]{1,0:T(8,128)}, u32[]{:S(2)}) copy-start(f32[1024,128]{1,0:T(8,128)} %get-tuple-element.9) | copy-start | bytes 1572868
  112.8 1.2 %copy-start = (f32[1024,128]{1,0:T(8,128)S(1)}, f32[1024,128]{1,0:T(8,128)}, u32[]{:S(2)}) copy-start(f32[1024,128]{1,0:T(8,128)} %get-tuple-element.10) | copy-start | bytes 1572868
  114.0 0.8 copy-start.2

commit v4 on v3

--- a/solution.py
+++ b/solution.py
@@ -44,7 +44,7 @@
 def kernel(
     dims,
     h_ref, u_ref, v_ref, cu_ref, cv_ref, idx_ref, wt_ref, val_ref, var_ref, cnt_ref, fc_ref,
-    ah_ref, au_ref, av_ref, fo_ref,
+    ana_ref, fo_ref,
     out_box, in_box, c_out, c_in, to_west, to_east, from_east, from_west,
     window, cour_u, cour_v, state, stencil, stencil_hi, stencil_lo, ana,
     back_out, back_in, inc_out, inc_in, h_in, u_in, v_in, c_edge, edges,
@@ -453,21 +453,23 @@
     coarse_i = lax.broadcasted_iota(jnp.int32, (LANES, 2 * LANES), 0)
     widen = jnp.where(lax.div(fine_i, 2) == coarse_i, 1.0, 0.0).astype(jnp.float32)
     for j in range(own_tiles):
-        at = slice(2 * j * LANES, 2 * (j + 1) * LANES)
         wide = dot(straight(inc_in[8 * j : 8 * j + 8])[0:64], widen, precision=HIGHEST)
         for var in range(3):
             for e in range(2):
-                fo_ref[var, e, 0:1, at] = fc_ref[var, e, 0:1, at] + wide[16 * var : 16 * var + 1]
+                for k in range(2):
+                    at = (2 * var + e) * 2 * own_tiles + 2 * j + k
+                    part = wide[16 * var : 16 * var + 1, k * LANES : (k + 1) * LANES]
+                    fo_ref[at : at + 1, :] = fc_ref[at : at + 1, :] + part
 
     for s in order:
         wait_bytes(back_in.at[s, pl.ds(0, n_reg - 1 if s == 0 else n_reg)], back_in_sem.at[s])
         first = lax.rem(a + s, n_mem) * own_tiles
 
         def unpack(j, carry):
-            for var, ref in enumerate((ah_ref, au_ref, av_ref)):
+            for var in range(3):
                 start = pl.multiple_of(j * 8, 8)
                 blocks = back_in[s, pl.ds(start, 8), var]
-                ref[pl.ds(first + j, MEMS, stride=tiles), :] = straight(blocks)[0:MEMS]
+                ana_ref[var, pl.ds(first + j, MEMS, stride=tiles), :] = straight(blocks)[0:MEMS]
             return carry
 
         lax.fori_loop(0, own_tiles, unpack, 0)
@@ -500,13 +502,16 @@
     cells = n_reg // 2 * COLS
     f32 = jnp.float32
     flat = (MEMS * tiles, LANES)
+    flat_fine = (fine.size // LANES, LANES)
     vmem = pl.BlockSpec(memory_space=pltpu.VMEM)
     dma = pltpu.SemaphoreType.DMA
     outs = pl.pallas_call(
         functools.partial(kernel, (n_mem, n_reg)),
-        out_shape=[jax.ShapeDtypeStruct(flat, f32)] * 3 + [jax.ShapeDtypeStruct(fine.shape, f32)],
+        out_shape=[
+            jax.ShapeDtypeStruct((3, *flat), f32), jax.ShapeDtypeStruct(flat_fine, f32),
+        ],
         in_specs=[pl.BlockSpec(memory_space=pl.ANY)] * 3 + [vmem] * 6 + [pl.BlockSpec(memory_space=pltpu.SMEM), vmem],
-        out_specs=[vmem] * 4,
+        out_specs=[vmem] * 2,
         scratch_shapes=[
             pltpu.VMEM((peers, 3, 8, LANES), f32),
             pltpu.VMEM((n_mem, n_reg, 3, 8, LANES), f32),
@@ -541,9 +546,9 @@
         h.reshape(flat), u.reshape(flat), v.reshape(flat),
         cu.reshape(tiles, LANES), cv.reshape(tiles, LANES),
         obs_index.transpose(0, 2, 1), obs_weight.transpose(0, 2, 1),
-        obs_value, obs_var, obs_count, fine,
+        obs_value, obs_var, obs_count, fine.reshape(flat_fine),
     )
-    return tuple(x.reshape(h.shape) for x in outs[:3]) + (outs[3],)
+    return tuple(outs[0][var].reshape(h.shape) for var in range(3)) + (outs[1].reshape(fine.shape),)
 
 
 def solution(mesh):

time: 116 us -> 115 us (level)
  local copies, waits for them, and re-layouts: 4.56 us -> 3.15 us
    unnamed x10 -> x3, local copies, waits for them, and re-layouts: 4.56 us -> 0.61 us
    slice x0 -> x1, local copies, waits for them, and re-layouts: none -> 2.53 us  [step(): outs[0][var].reshape(h.shape)]
where the time goes in v4:
time: 115 us; the launch traced here: 114 us
  Pallas kernels  110 us (96%)
  local copies, waits for them, and re-layouts  3.15 us (3%)
    pallas_call x1, Pallas kernels, step(): pl.pallas_call(functools.partial(kernel, (n_mem, n_reg)), out_shape=[jax....  110 us
    slice x1, local copies, waits for them, and re-layouts, step(): outs[0][var].reshape(h.shape)  2.53 us

profile of v4, /device:TPU:102, one launch (start us, length us, event | category | flops | bytes accessed | tf_op | source)
XLA Modules:
  0.0 114.0 jit_solution(16976199411127166234)
XLA Ops:
  0.6 110.2 %shard_map.138 = (f32[3,1024,128]{2,1,0:T(8,128)}, f32[48,128]{1,0:T(8,128)}) custom-call(f32[1024,128]{1,0:T(8,128)} %bitcast.12, f32[1024,128]{1,0:T(8,128)} %bitcast.13, f32[1024,128]{1,0:T(8,128)} %bitcast.14, f32[16,128]{1,0:T(8,128)} %bitcast.22, f32[16,128]{1,0:T(8,128)} %bitcast.23, s32[2,4,512]{2,1,0:T(4,128)} %bitcast.20, f32[2,4,512]{2,1,0:T(4,128)} %bitcast.21, ...), custom_call_target="tpu_custom_call" | custom-call | tf_op jit(solution)/shard_map/pallas_call | solution.py:508
  110.8 0.0 copy-start
  110.8 2.5 %fusion = (f32[1,1024,128]{2,1,0:T(8,128)}, f32[1,1024,128]{2,1,0:T(8,128)}, f32[1,1024,128]{2,1,0:T(8,128)}) fusion(f32[3,1024,128]{2,1,0:T(8,128)} %get-tuple-element.6), kind=kLoop, calls=%fused_computation | loop fusion | bytes 3145728 | tf_op jit(solution)/shard_map/slice | solution.py:551
  113.4 0.0 copy-done
  113.4 0.6 copy.20
Async XLA Ops:
  110.8 2.5 %copy-start = (f32[48,128]{1,0:T(8,128)S(1)}, f32[48,128]{1,0:T(8,128)}, u32[]{:S(2)}) copy-start(f32[48,128]{1,0:T(8,128)} %get-tuple-element.7) | copy-start | bytes 73732

commit v5 on v4

--- a/solution.py
+++ b/solution.py
@@ -43,11 +43,12 @@
 
 def kernel(
     dims,
-    h_ref, u_ref, v_ref, cu_ref, cv_ref, idx_ref, wt_ref, val_ref, var_ref, cnt_ref, fc_ref,
+    h_src, u_src, v_src, cu_src, cv_src, idx_src, wt_src, val_src, var_src, cnt_src, fc_src,
     ana_ref, fo_ref,
     out_box, in_box, c_out, c_in, to_west, to_east, from_east, from_west,
     window, cour_u, cour_v, state, stencil, stencil_hi, stencil_lo, ana,
     back_out, back_in, inc_out, inc_in, h_in, u_in, v_in, c_edge, edges,
+    cu_ref, cv_ref, idx_ref, wt_ref, val_ref, var_ref, cnt_ref, fc_ref,
     out_sem, in_sem, c_out_sem, c_in_sem, halo_out_sem, halo_in_sem,
     back_out_sem, back_in_sem, inc_out_sem, inc_in_sem, load_sem, edge_sem,
 ):
@@ -72,7 +73,11 @@
 
     loads = [
         pltpu.make_async_copy(ref, box, load_sem.at[i])
-        for i, (ref, box) in enumerate(((h_ref, h_in), (u_ref, u_in), (v_ref, v_in)))
+        for i, (ref, box) in enumerate((
+            (h_src, h_in), (u_src, u_in), (v_src, v_in), (cu_src, cu_ref), (cv_src, cv_ref),
+            (idx_src, idx_ref), (wt_src, wt_ref), (val_src, val_ref), (var_src, var_ref),
+            (cnt_src, cnt_ref), (fc_src, fc_ref),
+        ))
     ]
     for load in loads:
         load.start()
@@ -95,7 +100,7 @@
         lax.fori_loop(0, peers, greet_other_half, 0)
 
     lax.fori_loop(1, peers, greet, 0)
-    for load in loads:
+    for load in loads[:3]:
         load.wait()
 
     lane = lax.broadcasted_iota(jnp.int32, (8, LANES), 1)
@@ -115,12 +120,15 @@
 
     def pack(j, carry):
         for var, ref in enumerate((h_in, u_in, v_in)):
-            t = turned(ref[pl.ds(j, MEMS, stride=tiles), :])
+            pair = [ref[pl.ds(2 * j + k, MEMS, stride=tiles), :] for k in range(2)]
+            t = jnp.concatenate(pair, axis=0).T
             for k in range(8):
-                out_box[j * 8 + k, var] = t[COLS * k : COLS * k + 8]
+                x, y = t[COLS * k : COLS * k + 8], t[COLS * k + 8 : COLS * k + 16]
+                out_box[16 * j + k, var] = jnp.where(left, x, across(y))
+                out_box[16 * j + 8 + k, var] = jnp.where(left, across(x), y)
         return carry
 
-    lax.fori_loop(0, tiles, pack, 0)
+    lax.fori_loop(0, tiles // 2, pack, 0)
 
     def courant(j):
         cu = jnp.broadcast_to(cu_ref[pl.ds(j, 1), :], (32, LANES))
@@ -135,52 +143,38 @@
         c, u = across(c), across(u)
         return jnp.where(low, up(jnp.where(left, c, v)), jnp.where(left, u, h))
 
-    for j in range(own_tiles):
-        t = courant(a * own_tiles + j)
-        for k in range(8):
-            c_out[j * 8 + k] = t[COLS * k : COLS * k + 8]
-
-    c_edge[0] = courant(lax.rem(a + 1, n_mem) * own_tiles)[0:8]
-    c_edge[1] = courant(lax.rem(a * own_tiles + tiles - 1, tiles))[7 * COLS : 7 * COLS + 8]
-    for k in range(n_mem):
-        for kind, (m, c, going) in enumerate((
-            (k * n_reg + plane, c_out[plane], west_going),
-            ((k + 1) % n_mem * n_reg, c_edge[0], west_going),
-            (k * n_reg + plane - 1, c_out[plane - 1], east_going),
-            ((k * n_reg + peers - 1) % peers, c_edge[1], east_going),
-        )):
-            edges[k, kind] = going(out_box[m, 0], out_box[m, 1], out_box[m, 2], c)
-
     pl.semaphore_wait(barrier, peers + 1)
 
-    def send_courant(i, carry):
-        p = lax.rem(b + i, n_reg)
-        pltpu.make_async_remote_copy(
-            src_ref=c_out.at[p], dst_ref=c_in.at[b], send_sem=c_out_sem, recv_sem=c_in_sem,
-            device_id=(a, p, f), device_id_type=MESH,
-        ).start()
-        return carry
-
-    lax.fori_loop(1, n_reg, send_courant, 0)
-    c_in[b] = c_out[b]
-    in_box[0, b] = out_box[me]
-
-    for phase in phases:
-
-        def send_state(i, carry):
-            p_row = lax.rem(b + i, n_reg)
-            for s in phase:
-                p_mem = lax.rem(a + s, n_mem)
-                slot = (n_mem - s) % n_mem
-                pltpu.make_async_remote_copy(
-                    src_ref=out_box.at[p_mem * n_reg + p_row], dst_ref=in_box.at[slot, b],
-                    send_sem=out_sem, recv_sem=in_sem.at[slot],
-                    device_id=(p_mem, p_row, f), device_id_type=MESH,
-                ).start()
-            return carry
-
-        lax.fori_loop(1 if phase == [0] else 0, n_reg, send_state, 0)
-        for s in phase:
+    def send_rest():
+        for load in loads[3:]:
+            load.wait()
+        for j in range(own_tiles):
+            t = courant(a * own_tiles + j)
+            for k in range(8):
+                c_out[j * 8 + k] = t[COLS * k : COLS * k + 8]
+
+        c_edge[0] = courant(lax.rem(a + 1, n_mem) * own_tiles)[0:8]
+        c_edge[1] = courant(lax.rem(a * own_tiles + tiles - 1, tiles))[7 * COLS : 7 * COLS + 8]
+        for k in range(n_mem):
+            for kind, (m, c, going) in enumerate((
+                (k * n_reg + plane, c_out[plane], west_going),
+                ((k + 1) % n_mem * n_reg, c_edge[0], west_going),
+                (k * n_reg + plane - 1, c_out[plane - 1], east_going),
+                ((k * n_reg + peers - 1) % peers, c_edge[1], east_going),
+            )):
+                edges[k, kind] = going(out_box[m, 0], out_box[m, 1], out_box[m, 2], c)
+
+        def send_courant(i, carry):
+            p = lax.rem(b + i, n_reg)
+            pltpu.make_async_remote_copy(
+                src_ref=c_out.at[p], dst_ref=c_in.at[b], send_sem=c_out_sem, recv_sem=c_in_sem,
+                device_id=(a, p, f), device_id_type=MESH,
+            ).start()
+            return carry
+
+        lax.fori_loop(1, n_reg, send_courant, 0)
+        c_in[b] = c_out[b]
+        for s in order:
             p_mem = lax.rem(a + s, n_mem)
             slot = (n_mem - s) % n_mem
             for kind, (p_row, box, other) in enumerate((
@@ -204,6 +198,25 @@
                     pl.when(own)(stay.start)
                     pl.when(jnp.logical_not(own))(go.start)
 
+    in_box[0, b] = out_box[me]
+
+    for phase in phases:
+        if phase == phases[-1]:
+            send_rest()
+
+        def send_state(i, carry):
+            p_row = lax.rem(b + i, n_reg)
+            for s in phase:
+                p_mem = lax.rem(a + s, n_mem)
+                slot = (n_mem - s) % n_mem
+                pltpu.make_async_remote_copy(
+                    src_ref=out_box.at[p_mem * n_reg + p_row], dst_ref=in_box.at[slot, b],
+                    send_sem=out_sem, recv_sem=in_sem.at[slot],
+                    device_id=(p_mem, p_row, f), device_id_type=MESH,
+                ).start()
+            return carry
+
+        lax.fori_loop(1 if phase == [0] else 0, n_reg, send_state, 0)
     obs = idx_ref.shape[2]
     for q in range(2):
 
@@ -467,12 +480,16 @@
 
         def unpack(j, carry):
             for var in range(3):
-                start = pl.multiple_of(j * 8, 8)
-                blocks = back_in[s, pl.ds(start, 8), var]
-                ana_ref[var, pl.ds(first + j, MEMS, stride=tiles), :] = straight(blocks)[0:MEMS]
-            return carry
-
-        lax.fori_loop(0, own_tiles, unpack, 0)
+                x = back_in[s, pl.ds(pl.multiple_of(j * 16, 8), 8), var]
+                y = back_in[s, pl.ds(pl.multiple_of(j * 16 + 8, 8), 8), var]
+                rows = [jnp.where(left, x, across(y)), jnp.where(left, across(x), y)]
+                t = jnp.stack(rows, axis=1).reshape(LANES, LANES).T
+                for k in range(2):
+                    at = pl.ds(first + 2 * j + k, MEMS, stride=tiles)
+                    ana_ref[var, at, :] = t[k * MEMS : (k + 1) * MEMS]
+            return carry
+
+        lax.fori_loop(0, own_tiles // 2, unpack, 0)
 
     wait_bytes(c_out.at[pl.ds(0, n_reg - 1)], c_out_sem)
     wait_bytes(out_box.at[pl.ds(0, peers - 1)], out_sem)
@@ -510,7 +527,7 @@
         out_shape=[
             jax.ShapeDtypeStruct((3, *flat), f32), jax.ShapeDtypeStruct(flat_fine, f32),
         ],
-        in_specs=[pl.BlockSpec(memory_space=pl.ANY)] * 3 + [vmem] * 6 + [pl.BlockSpec(memory_space=pltpu.SMEM), vmem],
+        in_specs=[pl.BlockSpec(memory_space=pl.ANY)] * 11,
         out_specs=[vmem] * 2,
         scratch_shapes=[
             pltpu.VMEM((peers, 3, 8, LANES), f32),
@@ -536,8 +553,12 @@
             pltpu.VMEM(flat, f32), pltpu.VMEM(flat, f32), pltpu.VMEM(flat, f32),
             pltpu.VMEM((2, 8, LANES), f32),
             pltpu.VMEM((n_mem, 4, 8, LANES), f32),
+            pltpu.VMEM((tiles, LANES), f32), pltpu.VMEM((tiles, LANES), f32),
+            pltpu.VMEM((2, 4, obs), jnp.int32), pltpu.VMEM((2, 4, obs), f32),
+            pltpu.VMEM((2, obs), f32), pltpu.VMEM((2, obs), f32),
+            pltpu.SMEM((2,), jnp.int32), pltpu.VMEM(flat_fine, f32),
             dma, dma((n_mem,)), dma, dma, dma((2, n_mem)), dma((2, n_mem)),
-            dma, dma((n_mem,)), dma, dma, dma((3,)), dma,
+            dma, dma((n_mem,)), dma, dma, dma((11,)), dma,
         ],
         compiler_params=pltpu.CompilerParams(
             collective_id=0, has_side_effects=True, vmem_limit_bytes=56 * 1024 * 1024

time: 115 us -> 115 us (level)
  no operation moved by 1% of the time
where the time goes in v5:
time: 115 us; the launch traced here: 114 us
  Pallas kernels  110 us (96%)
  local copies, waits for them, and re-layouts  3.15 us (3%)
    pallas_call x1, Pallas kernels, step(): pl.pallas_call(functools.partial(kernel, (n_mem, n_reg)), out_shape=[jax....  110 us
    slice x1, local copies, waits for them, and re-layouts, step(): outs[0][var].reshape(h.shape)  2.53 us

profile of v5, /device:TPU:102, one launch (start us, length us, event | category | flops | bytes accessed | tf_op | source)
XLA Modules:
  0.0 113.9 jit_solution(12903997004516877730)
XLA Ops:
  0.6 110.1 %shard_map.138 = (f32[3,1024,128]{2,1,0:T(8,128)}, f32[48,128]{1,0:T(8,128)}) custom-call(f32[1024,128]{1,0:T(8,128)} %bitcast.12, f32[1024,128]{1,0:T(8,128)} %bitcast.13, f32[1024,128]{1,0:T(8,128)} %bitcast.14, f32[16,128]{1,0:T(8,128)} %bitcast.22, f32[16,128]{1,0:T(8,128)} %bitcast.23, s32[2,4,512]{2,1,0:T(4,128)} %bitcast.20, f32[2,4,512]{2,1,0:T(4,128)} %bitcast.21, ...), custom_call_target="tpu_custom_call" | custom-call | tf_op jit(solution)/shard_map/pallas_call | solution.py:525
  110.7 0.0 copy-start
  110.7 2.5 %fusion = (f32[1,1024,128]{2,1,0:T(8,128)}, f32[1,1024,128]{2,1,0:T(8,128)}, f32[1,1024,128]{2,1,0:T(8,128)}) fusion(f32[3,1024,128]{2,1,0:T(8,128)} %get-tuple-element.6), kind=kLoop, calls=%fused_computation | loop fusion | bytes 3145728 | tf_op jit(solution)/shard_map/slice | solution.py:572
  113.3 0.0 copy-done
  113.3 0.6 copy.20
Async XLA Ops:
  110.7 2.5 %copy-start = (f32[48,128]{1,0:T(8,128)S(1)}, f32[48,128]{1,0:T(8,128)}, u32[]{:S(2)}) copy-start(f32[48,128]{1,0:T(8,128)} %get-tuple-element.7) | copy-start | bytes 73732

commit v6 on v5

--- a/solution.py
+++ b/solution.py
@@ -356,12 +356,13 @@
     eye = jnp.where(row_i == col_i, 1.0, 0.0).astype(jnp.float32)
     obs_i = lax.broadcasted_iota(jnp.int32, (1, obs), 1)
 
-    for q in range(2):
+    for turn in range(2):
+        q = lax.rem(a + b + turn, 2)
         spreads, means = [], []
         obs_spread = jnp.zeros((members, obs), jnp.float32)
         mean_obs = jnp.zeros((1, obs), jnp.float32)
         for var in range(3):
-            x = state[var, q * half_rows : (q + 1) * half_rows].reshape(cells, members)
+            x = state[var, pl.ds(q * half_rows, half_rows)].reshape(cells, members)
             mean = jnp.sum(x, axis=1, keepdims=True) / members
             spread = split(x - mean)
             block = slice(var * cells, (var + 1) * cells)
@@ -371,11 +372,11 @@
             spreads.append(spread)
             means.append(mean)
         active = jnp.where(obs_i < cnt_ref[q], 1.0, 0.0)
-        weighted = obs_spread * (active / var_ref[q : q + 1, :])
+        weighted = obs_spread * (active / var_ref[pl.ds(q, 1), :])
         gram_sum = dot3(split(weighted), split(obs_spread), ((1,), (1,)))
         scaled = eye + gram_sum / (members - 1)
         fro = jnp.sqrt(all_sum(scaled * scaled))
-        innovation = jnp.sum(weighted * (val_ref[q : q + 1, :] - mean_obs), axis=1, keepdims=True)
+        innovation = jnp.sum(weighted * (val_ref[pl.ds(q, 1), :] - mean_obs), axis=1, keepdims=True)
         iterate = scaled / fro
         factor = split(1.5 * eye - 0.5 * iterate)
 
@@ -385,7 +386,7 @@
             return split(dot3(iterate, factor)), split(dot3(factor, root))
 
         iterate, root = lax.fori_loop(
-            1, NEWTON - 1, sweep, (split(dot3(split(iterate), factor)), factor), unroll=2
+            1, NEWTON - 1, sweep, (split(dot3(split(iterate), factor)), factor)
         )
         factor = split(1.5 * eye - 0.5 * dot3(root, iterate))
         transform = dot3(factor, root) / jnp.sqrt(fro)
@@ -416,7 +417,7 @@
                 y = ana[var, pl.ds(hi, 8), members:]
                 packed = jnp.where(lax.div(lax.rem(lane, MEMS), 16) == var, jnp.where(left, x, y), packed)
             inc_out[row] = packed
-            if q == 0:
+            if turn == 0:
                 send_inc(row)
                 for s in order:
                     send_back(s, row)
@@ -442,7 +443,7 @@
                 pl.when(row != b)(go.start)
 
         lax.fori_loop(0, half_rows, unload, 0)
-        if q:
+        if turn:
             for phase in phases:
 
                 def send_phase(i, carry):

time: 115 us -> 113 us (0.983)
  the two profiles are of different devices: /device:TPU:102 before, /device:TPU:1 now
where the time goes in v6:
time: 113 us; the launch traced here: 112 us
  Pallas kernels  109 us (96%)
  local copies, waits for them, and re-layouts  3.15 us (3%)
    pallas_call x1, Pallas kernels, step(): pl.pallas_call(functools.partial(kernel, (n_mem, n_reg)), out_shape=[jax....  109 us
    slice x1, local copies, waits for them, and re-layouts, step(): outs[0][var].reshape(h.shape)  2.53 us

profile of v6, /device:TPU:1, one launch (start us, length us, event | category | flops | bytes accessed | tf_op | source)
XLA Modules:
  0.0 112.5 jit_solution(1410208666360237456)
XLA Ops:
  0.6 108.7 %shard_map.138 = (f32[3,1024,128]{2,1,0:T(8,128)}, f32[48,128]{1,0:T(8,128)}) custom-call(f32[1024,128]{1,0:T(8,128)} %bitcast.12, f32[1024,128]{1,0:T(8,128)} %bitcast.13, f32[1024,128]{1,0:T(8,128)} %bitcast.14, f32[16,128]{1,0:T(8,128)} %bitcast.22, f32[16,128]{1,0:T(8,128)} %bitcast.23, s32[2,4,512]{2,1,0:T(4,128)} %bitcast.20, f32[2,4,512]{2,1,0:T(4,128)} %bitcast.21, ...), custom_call_target="tpu_custom_call" | custom-call | tf_op jit(solution)/shard_map/pallas_call | solution.py:526
  109.3 0.0 copy-start
  109.3 2.5 %fusion = (f32[1,1024,128]{2,1,0:T(8,128)}, f32[1,1024,128]{2,1,0:T(8,128)}, f32[1,1024,128]{2,1,0:T(8,128)}) fusion(f32[3,1024,128]{2,1,0:T(8,128)} %get-tuple-element.6), kind=kLoop, calls=%fused_computation | loop fusion | bytes 3145728 | tf_op jit(solution)/shard_map/slice | solution.py:573
  111.8 0.0 copy-done
  111.8 0.6 copy.20
Async XLA Ops:
  109.3 2.5 %copy-start = (f32[48,128]{1,0:T(8,128)S(1)}, f32[48,128]{1,0:T(8,128)}, u32[]{:S(2)}) copy-start(f32[48,128]{1,0:T(8,128)} %get-tuple-element.7) | copy-start | bytes 73732

commit v7 on v6

--- a/solution.py
+++ b/solution.py
@@ -444,11 +444,11 @@
 
         lax.fori_loop(0, half_rows, unload, 0)
         if turn:
-            for phase in phases:
+            for phase in phases[::-1]:
 
                 def send_phase(i, carry):
                     row = q * half_rows + lax.rem(b + i, half_rows)
-                    if phase == phases[0]:
+                    if phase == phases[-1]:
                         send_inc(row)
                     for s in phase:
                         send_back(s, row)
@@ -475,7 +475,7 @@
                     part = wide[16 * var : 16 * var + 1, k * LANES : (k + 1) * LANES]
                     fo_ref[at : at + 1, :] = fc_ref[at : at + 1, :] + part
 
-    for s in order:
+    for s in order[::-1]:
         wait_bytes(back_in.at[s, pl.ds(0, n_reg - 1 if s == 0 else n_reg)], back_in_sem.at[s])
         first = lax.rem(a + s, n_mem) * own_tiles
 

time: 113 us -> 114 us (level)
  the two profiles are of different devices: /device:TPU:1 before, /device:TPU:2 now
where the time goes in v7:
time: 114 us
  Pallas kernels  110 us (96%)
  local copies, waits for them, and re-layouts  3.15 us (3%)
    pallas_call x1, Pallas kernels, step(): pl.pallas_call(functools.partial(kernel, (n_mem, n_reg)), out_shape=[jax....  110 us
    slice x1, local copies, waits for them, and re-layouts, step(): outs[0][var].reshape(h.shape)  2.53 us

profile of v7, /device:TPU:2, one launch (start us, length us, event | category | flops | bytes accessed | tf_op | source)
XLA Modules:
  0.0 113.5 jit_solution(1841160030095725478)
XLA Ops:
  0.6 109.7 %shard_map.138 = (f32[3,1024,128]{2,1,0:T(8,128)}, f32[48,128]{1,0:T(8,128)}) custom-call(f32[1024,128]{1,0:T(8,128)} %bitcast.12, f32[1024,128]{1,0:T(8,128)} %bitcast.13, f32[1024,128]{1,0:T(8,128)} %bitcast.14, f32[16,128]{1,0:T(8,128)} %bitcast.22, f32[16,128]{1,0:T(8,128)} %bitcast.23, s32[2,4,512]{2,1,0:T(4,128)} %bitcast.20, f32[2,4,512]{2,1,0:T(4,128)} %bitcast.21, ...), custom_call_target="tpu_custom_call" | custom-call | tf_op jit(solution)/shard_map/pallas_call | solution.py:526
  110.4 0.0 copy-start
  110.4 2.5 %fusion = (f32[1,1024,128]{2,1,0:T(8,128)}, f32[1,1024,128]{2,1,0:T(8,128)}, f32[1,1024,128]{2,1,0:T(8,128)}) fusion(f32[3,1024,128]{2,1,0:T(8,128)} %get-tuple-element.6), kind=kLoop, calls=%fused_computation | loop fusion | bytes 3145728 | tf_op jit(solution)/shard_map/slice | solution.py:573
  112.9 0.0 copy-done
  112.9 0.6 copy.20
Async XLA Ops:
  110.4 2.5 %copy-start = (f32[48,128]{1,0:T(8,128)S(1)}, f32[48,128]{1,0:T(8,128)}, u32[]{:S(2)}) copy-start(f32[48,128]{1,0:T(8,128)} %get-tuple-element.7) | copy-start | bytes 73732
